TPU v7x, 256 devices: a whole 4x4x8 slice. The times are simulated.
256 devices in a mesh: ctx: 32 (over y, x, core), head: 8 (over z).
Axes of the slice: x: 4, y: 4, z: 8, core: 2. Of those that a mesh axis runs over, the one named last changes fastest.
Arguments:
- tokens: bfloat16 [8192, 4096], P('ctx', 'head'), may hold values from -6 to 6
- policy_weight: bfloat16 [3, 4096, 2048], P(None, 'ctx', 'head'), may hold values from -0.09375 to 0.09375
- reference_weight: bfloat16 [3, 4096, 2048], P(None, 'ctx', 'head'), may hold values from -0.09375 to 0.09375
Outputs:
- difference: float32 [8192, 2048], P('ctx', 'head')
- input_grad: float32 [8192, 4096], P('ctx', 'head')
All inputs are finite; a program needn't handle non-finite values.
Results may differ from a plain program's by a relative error of at most 0.0027.
Values may be sent and summed in bfloat16 or wider, within the bound.
A program may use at most 64 MiB of HBM per device.

v0:
```python
import math

import jax
import jax.numpy as jnp
from jax import lax
from jax.sharding import PartitionSpec as P

HD = 128


HIGH = lax.Precision.HIGHEST


def prefix(value, axis, join, neutral, backward):
    count, mine = (lax.axis_size(axis), lax.axis_index(axis))
    pieces = jax.tree.map(lambda part: lax.all_gather(part, axis), value)
    if backward:
        pieces = jax.tree.map(lambda part: part[::-1], pieces)
        mine = count - 1 - mine
    total = jax.tree.map(
        lambda part, zero: jnp.full_like(part, 0) + jnp.asarray(zero, part.dtype), value, neutral
    )

    def hop(position, total):
        longer = join(total, jax.tree.map(lambda part: part[position], pieces))
        return jax.tree.map(lambda new, old: jnp.where(position < mine, new, old), longer, total)

    return lax.fori_loop(0, count - 1, hop, total)


def per_device(tokens, policy_weight, reference_weight):
    row_count = tokens.shape[0]
    local_width = policy_weight.shape[2]
    heads_here = local_width // HD
    seq_tokens = row_count * lax.axis_size("ctx")
    out_scale = 1.0 / math.sqrt(HD * seq_tokens)
    whole = lax.all_gather(tokens, "head", axis=1, tiled=True)
    policy_whole = lax.all_gather(policy_weight, "ctx", axis=1, tiled=True)
    qkv_pol = jnp.einsum("td,cdj->tcj", whole, policy_whole, preferred_element_type=jnp.float32)
    qkv_ref = jnp.einsum(
        "tn,cnj->tcj",
        whole,
        lax.all_gather(reference_weight, "ctx", axis=1, tiled=True),
        preferred_element_type=jnp.float32,
    )

    def split_heads(qkv):
        return [qkv[:, slot].reshape(row_count, heads_here, HD) for slot in range(3)]

    query_pol, key_pol, value_pol = split_heads(qkv_pol)
    query_ref, key_ref, value_ref = split_heads(qkv_ref)
    causal = jnp.tril(jnp.ones((row_count, row_count), jnp.float32))

    def inner(query, keys, values):
        scores = jnp.einsum("thd,shd->hts", query, keys, precision=HIGH) * causal
        return (scores, jnp.einsum("hts,shd->thd", scores, values, precision=HIGH))

    scores_pol, local_pol = inner(query_pol, key_pol, value_pol)
    _, local_ref = inner(query_ref, key_ref, value_ref)
    own_pol = jnp.einsum("thd,the->hde", key_pol, value_pol, precision=HIGH)
    own_ref = jnp.einsum("thd,the->hde", key_ref, value_ref, precision=HIGH)
    zeros = jnp.zeros((heads_here, HD, HD), jnp.float32)

    def add_pair(earlier, later):
        return (earlier[0] + later[0], earlier[1] + later[1])

    prefix_pol, prefix_ref = prefix((own_pol, own_ref), "ctx", add_pair, (zeros, zeros), False)
    out_pol = out_scale * (
        local_pol + jnp.einsum("thd,hde->the", query_pol, prefix_pol, precision=HIGH)
    )
    out_ref = out_scale * (
        local_ref + jnp.einsum("thd,hde->the", query_ref, prefix_ref, precision=HIGH)
    )
    difference = out_pol - out_ref
    weighted = jnp.einsum("thd,shd->hts", difference, value_pol, precision=HIGH) * causal
    grad_query = jnp.einsum("hts,shd->thd", weighted, key_pol, precision=HIGH)
    grad_query = out_scale * (
        grad_query + jnp.einsum("the,hde->thd", difference, prefix_pol, precision=HIGH)
    )
    later_own = jnp.einsum("thd,the->hde", query_pol, difference, precision=HIGH)
    suffix = prefix(later_own, "ctx", lambda earlier, later: earlier + later, zeros, True)
    grad_key = jnp.einsum("hts,thd->shd", weighted, query_pol, precision=HIGH)
    grad_key = out_scale * (
        grad_key + jnp.einsum("hde,she->shd", suffix, value_pol, precision=HIGH)
    )
    grad_value = jnp.einsum("hts,the->she", scores_pol, difference, precision=HIGH)
    grad_value = out_scale * (
        grad_value + jnp.einsum("hde,shd->she", suffix, key_pol, precision=HIGH)
    )
    grad_qkv = (
        jnp.stack([grad_query, grad_key, grad_value], 1)
        .reshape(row_count, 3, local_width)
        .astype(jnp.bfloat16)
    )
    partial_grad = jnp.einsum(
        "tcj,cdj->td", grad_qkv, policy_whole, preferred_element_type=jnp.float32
    )
    input_grad = lax.psum_scatter(partial_grad, "head", scatter_dimension=1, tiled=True)
    return (difference.reshape(row_count, local_width), input_grad)


def solution(mesh):
    in_specs = (P("ctx", "head"), P(None, "ctx", "head"), P(None, "ctx", "head"))
    out_specs = (P("ctx", "head"), P("ctx", "head"))
    return jax.shard_map(
        per_device, mesh=mesh, in_specs=in_specs, out_specs=out_specs, check_vma=False
    )
```

profile of v0, /device:TPU:1, one launch (start us, length us, event | category | flops | bytes accessed | tf_op | source)
XLA Modules:
  0.0 476.0 jit_solution(5663304150087823383)
XLA Ops:
  7.9 1.7 copy.27
  9.8 1.7 copy.31
  11.6 39.5 %all-gather.10.cloned.1.call-done = bf16[256,4096]{1,0:T(8,128)(2,1)} async-done(((bf16[256,512]{1,0:T(8,128)(2,1)}), bf16[256,4096]{1,0:T(8,128)(2,1)}) %all-gather.10.cloned.1.call-update) | async-done | bytes 2097168 | tf_op jit(solution)/shard_map/all_gather | solution.py:37
  51.0 65.1 %all-gather.12.cloned.1.call-done = bf16[3,4096,256]{1,2,0:T(8,128)(2,1)} async-done(((bf16[3,128,256]{1,2,0:T(8,128)(2,1)}), bf16[3,4096,256]{1,2,0:T(8,128)(2,1)}) %all-gather.12.cloned.1.call-update) | async-done | bytes 6291472 | tf_op jit(solution)/shard_map/all_gather | solution.py:38
  116.2 5.2 %fusion.2 = f32[256,3,256]{0,2,1:T(8,128)S(1)} fusion(bf16[3,4096,256]{1,2,0:T(8,128)(2,1)} %all-gather.12.cloned.1.call-done, bf16[256,4096]{1,0:T(8,128)(2,1)} %all-gather.10.cloned.1.call-done), kind=kOutput, calls=%fused_computation.6 | convolution fusion | flops 1610612736 | bytes 9175040 | tf_op jit(solution)/shard_map/td,cdj->tcj/dot_general | solution.py:39
  122.6 55.7 %all-gather.14.cloned.1.call-done = bf16[3,4096,256]{1,2,0:T(8,128)(2,1)} async-done(((bf16[3,128,256]{1,2,0:T(8,128)(2,1)}), bf16[3,4096,256]{1,2,0:T(8,128)(2,1)}) %all-gather.14.cloned.1.call-update) | async-done | bytes 6291472 | tf_op jit(solution)/shard_map/all_gather | solution.py:43
  178.3 5.2 %fusion = f32[256,3,256]{0,2,1:T(8,128)S(1)} fusion(bf16[3,4096,256]{1,2,0:T(8,128)(2,1)} %all-gather.14.cloned.1.call-done, bf16[256,4096]{1,0:T(8,128)(2,1)} %all-gather.10.cloned.1.call-done), kind=kOutput, calls=%fused_computation.4 | convolution fusion | flops 1610612736 | bytes 9175040 | tf_op jit(solution)/shard_map/tn,cnj->tcj/dot_general | solution.py:40
  187.4 44.7 %all-gather.16.cloned.1.call-done = f32[64,128,128]{2,1,0:T(8,128)} async-done(((f32[2,128,128]{2,1,0:T(8,128)}), f32[64,128,128]{2,1,0:T(8,128)}) %all-gather.16.cloned.1.call-update) | async-done | bytes 4194320 | tf_op jit(solution)/shard_map/all_gather | solution.py:16
  232.1 53.5 %all-gather.18.cloned.1.call-done = f32[64,128,128]{2,1,0:T(8,128)} async-done(((f32[2,128,128]{2,1,0:T(8,128)}), f32[64,128,128]{2,1,0:T(8,128)}) %all-gather.18.cloned.1.call-update) | async-done | bytes 4194320 | tf_op jit(solution)/shard_map/all_gather | solution.py:16
  285.6 33.7 %while.30 = (s32[]{:T(128)}, f32[2,128,128]{2,1,0:T(8,128)S(1)}, f32[2,128,128]{2,1,0:T(8,128)S(1)}, s32[]{:T(128)}, f32[32,2,128,128]{3,2,1,0:T(8,128)}, /*index=5*/f32[32,2,128,128]{3,2,1,0:T(8,128)}, s32[]{:T(128)}, s32[]{:T(128)}) while((s32[]{:T(128)}, f32[2,128,128]{2,1,0:T(8,128)S(1)}, f32[2,128,128]{2,1,0:T(8,128)S(1)}, ...), condition=%wide.region_1.2_spmd.clone, body=%wide.region_0.1_spmd.clone.sunk | while | flops 196612 | bytes 786549 | solution.py:28
  286.7 1.1 add_select_fusion.5
  287.8 1.1 add_select_fusion.5
  288.9 1.1 add_select_fusion.5
  290.0 1.1 add_select_fusion.5
  291.0 1.1 add_select_fusion.5
  292.1 1.1 add_select_fusion.5
  293.2 1.1 add_select_fusion.5
  294.3 1.1 add_select_fusion.5
  295.4 1.1 add_select_fusion.5
  296.5 1.1 add_select_fusion.5
  297.6 1.1 add_select_fusion.5
  298.7 1.1 add_select_fusion.5
  299.8 1.1 add_select_fusion.5
  304.1 1.1 add_select_fusion.5
  305.2 1.1 add_select_fusion.5
  306.3 1.1 add_select_fusion.5
  307.4 1.1 add_select_fusion.5
  324.2 47.8 %all-gather.20.cloned.1.call-done = f32[64,128,128]{2,1,0:T(8,128)} async-done(((f32[2,128,128]{2,1,0:T(8,128)}), f32[64,128,128]{2,1,0:T(8,128)}) %all-gather.20.cloned.1.call-update) | async-done | bytes 4194320 | tf_op jit(solution)/shard_map/all_gather | solution.py:16
  372.0 4.8 %rev.3 = f32[32,2,128,128]{3,2,1,0:T(8,128)} reverse(f32[32,2,128,128]{3,2,1,0:T(8,128)} %bitcast.106), dimensions={0} | reverse | bytes 8388608 | tf_op jit(solution)/shard_map/rev | solution.py:18
  376.8 30.1 %while.31 = (s32[]{:T(128)}, f32[2,128,128]{2,1,0:T(8,128)S(1)}, s32[]{:T(128)}, f32[32,2,128,128]{3,2,1,0:T(8,128)}, s32[]{:T(128)}, /*index=5*/s32[]{:T(128)}) while((s32[]{:T(128)}, f32[2,128,128]{2,1,0:T(8,128)S(1)}, s32[]{:T(128)}, f32[32,2,128,128]{3,2,1,0:T(8,128)}, s32[]{:T(128)}, /*index=5*/s32[]{:T(128)}) %tuple.75), condition=%wide.region_3.4_spmd.clone, body=%wide.region_2.3_spmd.clone.sunk | while | flops 98308 | bytes 393317 | solution.py:28
  407.9 6.6 %convolution_bitcast_fusion = f32[256,4096]{1,0:T(8,128)} fusion(bf16[3,4096,256]{1,2,0:T(8,128)(2,1)} %all-gather.12.cloned.1.call-done, bf16[256,1,256]{2,0,1:T(8,128)(2,1)S(1)} %copy.46, bf16[256,1,256]{2,0,1:T(8,128)(2,1)S(1)} %copy.45, bf16[256,1,256]{2,0,1:T(8,128)(2,1)S(1)} %copy.44), kind=kOutput, calls=%fused_computation.3 | convolution fusion | flops 1611005952 | bytes 10878976 | tf_op jit(solution)/shard_map/tcj,cdj->td/dot_general | solution.py:95
  415.5 53.7 %reduce-scatter.2.cloned.1.call-done = f32[256,512]{1,0:T(8,128)} async-done(((f32[256,4096]{1,0:T(8,128)}), f32[256,512]{1,0:T(8,128)}) %reduce-scatter.2.cloned.1.call-update) | async-done | bytes 524304 | tf_op jit(solution)/shard_map/reduce_scatter | solution.py:98
  (85 shorter events, 56.8 us)
Async XLA Ops:
  7.2 43.9 %all-gather.10.cloned.1.call-start = ((), (), s32[]{:S(2)}) async-start(), calls=%async_computation.1 | async-start | bytes 2359296 | tf_op jit(solution)/shard_map/all_gather | solution.py:37
  7.9 108.3 %all-gather.12.cloned.1.call-start = ((), (), s32[]{:S(2)}) async-start(), calls=%async_computation.2 | async-start | bytes 6488064 | tf_op jit(solution)/shard_map/all_gather | solution.py:38
  9.7 168.6 %all-gather.14.cloned.1.call-start = ((), (), s32[]{:S(2)}) async-start(), calls=%async_computation.3 | async-start | bytes 6488064 | tf_op jit(solution)/shard_map/all_gather | solution.py:43
  11.5 220.6 %all-gather.16.cloned.1.call-start = ((), (), s32[]{:S(2)}) async-start(), calls=%async_computation.5 | async-start | bytes 4325376 | tf_op jit(solution)/shard_map/all_gather | solution.py:16
  122.5 163.1 %all-gather.18.cloned.1.call-start = ((), (), s32[]{:S(2)}) async-start(), calls=%async_computation.6 | async-start | bytes 4325376 | tf_op jit(solution)/shard_map/all_gather | solution.py:16
  184.7 187.3 %all-gather.20.cloned.1.call-start = ((), (), s32[]{:S(2)}) async-start(), calls=%async_computation.7 | async-start | bytes 4325376 | tf_op jit(solution)/shard_map/all_gather | solution.py:16
  321.3 147.8 %reduce-scatter.2.cloned.1.call-start = ((), (), s32[]{:S(2)}) async-start(), calls=%async_computation.4 | async-start | bytes 4718592 | tf_op jit(solution)/shard_map/reduce_scatter | solution.py:98
Sparse Core Ops, SparseCore 0:
  9.8 41.2 all-gather.9
  54.1 62.0 all-gather.11
  119.2 59.0 all-gather.13
  181.3 50.7 all-gather.15
  235.1 50.5 all-gather.17
  321.4 50.5 all-gather.19
  414.7 54.3 reduce-scatter.1
where the time goes:
time: 477 us; the launch traced here: 476 us
  waiting for transfers between devices  361 us (76%)
  other arithmetic  62.5 us (13%)
  matrix products  27 us (6%)
  between operations  14.3 us (3%)
  local copies, waits for them, and re-layouts  9.49 us (2%)
    all_gather x3, waiting for transfers between devices, prefix(): pieces = jax.tree.map(lambda part: lax.all_gather(part, axis), value)  146 us
    all_gather x1, waiting for transfers between devices, per_device(): policy_whole = lax.all_gather(policy_weight, 'ctx', axis=1, tiled=True)  65.1 us
    select_n x62, other arithmetic, hop(): jnp.where(position < mine, new, old)  62.4 us
    all_gather x1, waiting for transfers between devices, per_device(): lax.all_gather(reference_weight, 'ctx', axis=1, tiled=True)  55.7 us
    reduce_scatter x1, waiting for transfers between devices, per_device(): lax.psum_scatter(partial_grad, 'head', scatter_dimension=1, tiled=True)  53.7 us
    all_gather x1, waiting for transfers between devices, per_device(): whole = lax.all_gather(tokens, 'head', axis=1, tiled=True)  39.5 us
  transfers between devices with their start and end apart: 7, of which 7 were waited for; matrix products, arithmetic and copies ran while one was open for 5% of the time, Pallas kernels for 0%

commit v1 on v0

v1 whole, which is shorter than its diff:
```python
import functools
import math

import jax
import jax.numpy as jnp
from jax import lax
from jax.experimental import pallas as pl
from jax.experimental.pallas import tpu as pltpu
from jax.sharding import PartitionSpec as P

HD = 128
F32 = jnp.float32
BF16 = jnp.bfloat16
MESH = pl.DeviceIdType.MESH

PIECES = ((0, 1), (0, 2), (1, 1), (1, 2), (0, 0), (1, 0))
KP, VP, KR, VR, QP, QR = range(6)


def mm(a, b, ca, cb):
    return lax.dot_general(a, b, (((ca,), (cb,)), ((), ())), preferred_element_type=F32)


def split(a):
    high = a.astype(BF16)
    return high, (a - high.astype(F32)).astype(BF16)


def mm3(a, b, ca, cb):
    return mm(a[0], b[0], ca, cb) + (mm(a[0], b[1], ca, cb) + mm(a[1], b[0], ca, cb))


def kernel(
    scale, tok_ref, pol_ref, ref_ref, diff_ref, grad_ref,
    w, xs, acc, g, own_f, sib_f, chip_f, row_f, tot_f, col_f, fin_f, got_f, pre_f,
    own_b, sib_b, chip_b, row_b, tot_b, col_b, fin_b, got_b, pre_b,
    out_r, in_r, out_l, in_l,
    local_sem, p1_send, p1_recv, p2_send, p2_recv, sib_send, sib_recv,
    tok_send, tok_recv, pre_send, pre_recv, rs_send, rs_recv,
):
    ctx, z = lax.axis_index("ctx"), lax.axis_index("head")
    y, x, k = ctx // 8, lax.rem(ctx // 2, 4), lax.rem(ctx, 2)
    zs = lax.axis_size("head")

    def at(yy, xx, kk):
        return ((yy * 4 + xx) * 2 + kk, z)

    def turn(i, by):
        return lax.rem(i + by + 4, 4)

    xdev = [at(y, turn(x, d), k) for d in range(4)]
    ydev = [at(turn(y, d), x, k) for d in range(4)]
    sibling = at(y, x, 1 - k)
    zr, zl = (ctx, lax.rem(z + 1, zs)), (ctx, lax.rem(z + zs - 1, zs))

    def zb(by):
        return lax.rem(z + by + zs, zs)

    barrier = pltpu.get_barrier_semaphore()
    greeted = xdev[1:] + ydev[1:] + [sibling, zr, zl]
    for dev in greeted:
        pl.semaphore_signal(barrier, inc=1, device_id=dev, device_id_type=MESH)
    pl.semaphore_wait(barrier, len(greeted))

    sent = []

    def send(src, dst, ssem, rsem, dev):
        copy = pltpu.make_async_remote_copy(
            src_ref=src, dst_ref=dst, send_sem=ssem, recv_sem=rsem,
            device_id=dev, device_id_type=MESH,
        )
        copy.start()
        sent.append(copy)

    def arrived(dst, sem):
        pltpu.make_async_remote_copy(
            src_ref=dst, dst_ref=dst, send_sem=sem, recv_sem=sem,
            device_id=sibling, device_id_type=MESH,
        ).wait_recv()

    def source(s):
        model, slot = PIECES[s]
        return (pol_ref, ref_ref)[model].at[slot]

    def block(s, i, j):
        return w.at[s, j, i, k] if s % 2 == 0 else w.at[s, i, j, k]

    def part(s, i, j, half):
        rows = pl.ds(64 * half, 64)
        return w.at[s, j, i, k, rows] if s % 2 == 0 else w.at[s, i, j, k, rows]

    def group(s, j, kk):
        return w.at[s, j, :, kk] if s % 2 == 0 else w.at[s, :, j, kk]

    def some(s, j, half):
        few = pl.ds(2 * half, 2)
        return w.at[s, j, few, k] if s % 2 == 0 else w.at[s, few, j, k]

    def axes(s):
        return (x, y, xdev, ydev) if s % 2 == 0 else (y, x, ydev, xdev)

    def p1_start(stage):
        for s in (2 * stage, 2 * stage + 1):
            i, j, first, _ = axes(s)
            for n, d in ((0, 1), (1, 3)):
                send(source(s), block(s, i, j), p1_send.at[s, n], p1_recv.at[s, n], first[d])

    def p1_forward(stage):
        for n, d, to in ((0, -1, 1), (1, 1, 3)):
            for s in (2 * stage, 2 * stage + 1):
                i, j, first, _ = axes(s)
                arrived(block(s, turn(i, d), j), p1_recv.at[s, n])
                half = part(s, turn(i, d), j, n)
                send(half, half, p1_send.at[s, 2 + n], p1_recv.at[s, 2 + n], first[to])

    def p2_start(stage):
        for s in (2 * stage, 2 * stage + 1):
            i, j, first, second = axes(s)
            for n in range(2):
                arrived(part(s, turn(i, 2), j, n), p1_recv.at[s, 2 + n])
            mine = group(s, j, k)
            for n, d in ((0, 1), (1, 3)):
                send(mine, mine, p2_send.at[s, n], p2_recv.at[s, n], second[d])
        for s in (2 * stage, 2 * stage + 1):
            mine = group(s, axes(s)[1], k)
            send(mine, mine, sib_send.at[s, 0], sib_recv.at[s, 0], sibling)

    def p2_forward(stage):
        for n, d, to in ((0, -1, 1), (1, 1, 3)):
            for s in (2 * stage, 2 * stage + 1):
                i, j, _, second = axes(s)
                theirs = group(s, turn(j, d), k)
                arrived(theirs, p2_recv.at[s, n])
                half = some(s, turn(j, d), n)
                send(half, half, p2_send.at[s, 2 + n], p2_recv.at[s, 2 + n], second[to])
                send(theirs, theirs, sib_send.at[s, 1 + n], sib_recv.at[s, 1 + n], sibling)

    def p2_done(stage):
        for s in (2 * stage, 2 * stage + 1):
            j = axes(s)[1]
            for n in range(2):
                arrived(some(s, turn(j, 2), n), p2_recv.at[s, 2 + n])
            theirs = group(s, turn(j, 2), k)
            send(theirs, theirs, sib_send.at[s, 3], sib_recv.at[s, 3], sibling)

    def sib_done(stage):
        for s in (2 * stage, 2 * stage + 1):
            j = axes(s)[1]
            for n, d in ((0, 0), (1, -1), (2, 1), (3, 2)):
                arrived(group(s, turn(j, d), 1 - k), sib_recv.at[s, n])

    def tok(by):
        return xs.at[zb(by)]

    def tok_half(by, half):
        return xs.at[zb(by), pl.ds(128 * half, 128)]

    def tok_start():
        send(tok_ref, tok(0), tok_send.at[0, 0], tok_recv.at[0, 0], zr)
        send(tok_ref, tok(0), tok_send.at[1, 0], tok_recv.at[1, 0], zl)

    def tok_forward(step):
        for n, by, to in ((0, -step, zr), (1, step, zl)):
            arrived(tok(by), tok_recv.at[n, step - 1])
            src = tok(by) if step < 3 else tok_half(by, n)
            send(src, src, tok_send.at[n, step], tok_recv.at[n, step], to)

    def tok_done():
        for n in range(2):
            arrived(tok_half(4, n), tok_recv.at[n, 3])

    def rows_of(s, h):
        return w[s, h // 2, pl.ds(2 * lax.rem(h, 2), 2)].reshape(512, 256)

    def project(stage):
        for s in (2 * stage, 2 * stage + 1):
            acc[s] = jnp.zeros((256, 256), F32)

            @pl.loop(0, 8)
            def _(h):
                acc[s] += mm(xs[h], rows_of(s, h), 1, 0)

    def head(s, hh):
        return acc[s, :, hh * HD:(hh + 1) * HD]

    def sum_start(turn_at, own, sib):
        send(own.at[1 - k], sib, pre_send.at[turn_at, 0], pre_recv.at[turn_at, 0], sibling)

    def sum_x(turn_at, own, sib, chip, row):
        arrived(sib, pre_recv.at[turn_at, 0])
        chip[...] = own[k] + sib[...]
        for d in (2, 1, 3):
            send(chip, row.at[x], pre_send.at[turn_at, d], pre_recv.at[turn_at, d], xdev[d])

    def sum_y(turn_at, chip, row, tot, col, pre, before):
        total = chip[...]
        partial = jnp.zeros_like(total)
        for d in (1, 3, 2):
            at_x = turn(x, -d)
            arrived(row.at[at_x], pre_recv.at[turn_at, d])
            value = row[at_x]
            total += value
            partial += jnp.where(before(at_x, x), value, 0.0)
        tot[...] = total
        for d in (2, 1, 3):
            send(tot, col.at[y], pre_send.at[turn_at, 3 + d], pre_recv.at[turn_at, 3 + d], ydev[d])
        pre[...] = partial

    def sum_end(turn_at, own, sib, col, fin, got, pre, before, last):
        total = pre[...]
        for d in (1, 3, 2):
            at_y = turn(y, -d)
            arrived(col.at[at_y], pre_recv.at[turn_at, 3 + d])
            total += jnp.where(before(at_y, y), col[at_y], 0.0)
        fin[...] = total + jnp.where(k != last, own[k], 0.0)
        send(fin, got, pre_send.at[turn_at, 7], pre_recv.at[turn_at, 7], sibling)
        pre[...] = total + jnp.where(k == last, sib[...], 0.0)
        arrived(got, pre_recv.at[turn_at, 7])

    for s in range(6):
        pltpu.make_async_copy(source(s), w.at[s, y, x, k], local_sem.at[s]).start()
    pltpu.make_async_copy(tok_ref, tok(0), local_sem.at[6]).start()
    p1_start(0)
    tok_start()
    for s in range(6):
        pltpu.make_async_copy(source(s), w.at[s, y, x, k], local_sem.at[s]).wait()
    pltpu.make_async_copy(tok_ref, tok(0), local_sem.at[6]).wait()
    p1_forward(0)
    p2_start(0)
    p1_start(1)
    tok_forward(1)
    p2_forward(0)
    p1_forward(1)
    tok_forward(2)
    p2_done(0)
    p2_start(1)
    p1_start(2)
    tok_forward(3)
    p2_forward(1)
    p1_forward(2)
    p2_done(1)
    p2_start(2)
    tok_done()
    sib_done(0)
    project(0)
    for hh in range(2):
        own_f[hh, 0] = mm3(split(head(KP, hh)), split(head(VP, hh)), 0, 0)
    sib_done(1)
    project(1)
    for hh in range(2):
        own_f[hh, 1] = mm3(split(head(KR, hh)), split(head(VR, hh)), 0, 0)
    earlier = lambda a, b: a < b
    later = lambda a, b: a > b
    sum_start(0, own_f, sib_f)
    p2_forward(2)
    sum_x(0, own_f, sib_f, chip_f, row_f)
    p2_done(2)
    sum_y(0, chip_f, row_f, tot_f, col_f, pre_f, earlier)
    sib_done(2)
    project(2)
    sum_end(0, own_f, sib_f, col_f, fin_f, got_f, pre_f, earlier, 1)

    rows = lax.broadcasted_iota(jnp.int32, (256, 256), 0)
    columns = lax.broadcasted_iota(jnp.int32, (256, 256), 1)
    causal = rows >= columns

    def prefix(model, hh):
        return jnp.where(k == hh, pre_f[model], got_f[model])

    for hh in range(2):
        cols = slice(hh * HD, (hh + 1) * HD)
        outs = []
        for model, (qs, ks, vs) in enumerate(((QP, KP, VP), (QR, KR, VR))):
            q, kk, v = (split(head(s, hh)) for s in (qs, ks, vs))
            scores = split(jnp.where(causal, mm3(q, kk, 1, 1), 0.0))
            outs.append(
                scale * (mm3(scores, v, 1, 0) + mm3(q, split(prefix(model, hh)), 1, 0))
            )
        diff = outs[0] - outs[1]
        diff_ref[:, cols] = diff
        own_b[hh] = mm3(split(head(QP, hh)), split(diff), 0, 0)
    sum_start(1, own_b, sib_b)
    sum_x(1, own_b, sib_b, chip_b, row_b)

    for hh in range(2):
        cols = slice(hh * HD, (hh + 1) * HD)
        q, kk, v = (split(head(s, hh)) for s in (QP, KP, VP))
        diff = split(diff_ref[:, cols])
        weighted = split(jnp.where(causal, mm3(diff, v, 1, 1), 0.0))
        scores = split(jnp.where(causal, mm3(q, kk, 1, 1), 0.0))
        dq = mm3(weighted, kk, 1, 0) + mm3(diff, split(prefix(0, hh)), 1, 1)
        g[0, :, cols] = (scale * dq).astype(BF16)
        acc[KR, :, cols] = mm3(weighted, q, 0, 0)
        acc[VR, :, cols] = mm3(scores, diff, 0, 0)
        if hh == 0:
            sum_y(1, chip_b, row_b, tot_b, col_b, pre_b, later)
    sum_end(1, own_b, sib_b, col_b, fin_b, got_b, pre_b, later, 0)
    for hh in range(2):
        cols = slice(hh * HD, (hh + 1) * HD)
        kk, v = (split(head(s, hh)) for s in (KP, VP))
        suffix = split(jnp.where(k == hh, pre_b[...], got_b[...]))
        g[1, :, cols] = (scale * (acc[KR, :, cols] + mm3(v, suffix, 1, 1))).astype(BF16)
        g[2, :, cols] = (scale * (acc[VR, :, cols] + mm3(kk, suffix, 1, 0))).astype(BF16)

    def term(by, half):
        h, few = zb(by), slice(128 * half, 128 * half + 128)
        return (
            mm(g[0, few], rows_of(QP, h), 1, 1)
            + mm(g[1, few], rows_of(KP, h), 1, 1)
            + mm(g[2, few], rows_of(VP, h), 1, 1)
        )

    def hop(n, sign, out, inn, to, step, half):
        value = term(sign * (5 - step), half)
        fresh = step == 1 or (step == 2 and half != n)
        if not fresh:
            arrived(inn.at[step - 2, half], rs_recv.at[n, step - 2, half])
            value = value + inn[step - 2, half].astype(F32)
        out[step - 1, half] = value.astype(BF16)
        send(
            out.at[step - 1, half], inn.at[step - 1, half],
            rs_send.at[n, step - 1, half], rs_recv.at[n, step - 1, half], to,
        )

    ways = ((0, 1, out_r, in_r, zr), (1, -1, out_l, in_l, zl))
    for step in range(1, 5):
        for turn_at in range(2):
            for n, sign, out, inn, to in ways:
                half = (1 - n) if turn_at == 0 else n
                if step == 1 and half != n:
                    continue
                hop(n, sign, out, inn, to, step, half)
    for half in range(2):
        few = slice(128 * half, 128 * half + 128)
        grad_ref[few] = term(0, half)
    for turn_at in range(2):
        for n, _, _, inn, _ in ways:
            half = (1 - n) if turn_at == 0 else n
            few = slice(128 * half, 128 * half + 128)
            arrived(inn.at[3, half], rs_recv.at[n, 3, half])
            grad_ref[few] += inn[3, half].astype(F32)
    for copy in sent:
        copy.wait_send()


def per_device(tokens, policy_weight, reference_weight):
    seq = tokens.shape[0] * lax.axis_size("ctx")
    scale = 1.0 / math.sqrt(HD * seq)
    state = lambda *lead: pltpu.VMEM((*lead, HD, HD), F32)
    half = pltpu.VMEM((4, 2, 128, 512), BF16)
    dma = pltpu.SemaphoreType.DMA
    return pl.pallas_call(
        functools.partial(kernel, scale),
        out_shape=(
            jax.ShapeDtypeStruct((256, 256), F32),
            jax.ShapeDtypeStruct((256, 512), F32),
        ),
        in_specs=[pl.BlockSpec(memory_space=pl.ANY)] * 3,
        out_specs=[pl.BlockSpec(memory_space=pltpu.VMEM)] * 2,
        scratch_shapes=[
            pltpu.VMEM((6, 4, 4, 2, 128, 256), BF16),
            pltpu.VMEM((8, 256, 512), BF16),
            pltpu.VMEM((6, 256, 256), F32),
            pltpu.VMEM((3, 256, 256), BF16),
            state(2, 2), state(2), state(2), state(4, 2), state(2), state(4, 2),
            state(2), state(2), state(2),
            state(2), state(), state(), state(4), state(), state(4), state(), state(), state(),
            half, half, half, half,
            dma((7,)), dma((6, 4)), dma((6, 4)), dma((6, 4)), dma((6, 4)),
            dma((6, 4)), dma((6, 4)), dma((2, 4)), dma((2, 4)), dma((2, 8)), dma((2, 8)),
            dma((2, 4, 2)), dma((2, 4, 2)),
        ],
        compiler_params=pltpu.CompilerParams(
            collective_id=0, has_side_effects=True, vmem_limit_bytes=58 * 2**20
        ),
    )(tokens, policy_weight, reference_weight)


def solution(mesh):
    in_specs = (P("ctx", "head"), P(None, "ctx", "head"), P(None, "ctx", "head"))
    out_specs = (P("ctx", "head"), P("ctx", "head"))
    return jax.shard_map(
        per_device, mesh=mesh, in_specs=in_specs, out_specs=out_specs, check_vma=False
    )
```

time: 477 us -> 115 us (0.24)
  waiting for transfers between devices: 361 us -> 0 us
  Pallas kernels: 0 us -> 112 us
  other arithmetic: 62.5 us -> 0 us
  matrix products: 27 us -> 0 us
  between operations: 14.3 us -> 0.65 us
  local copies, waits for them, and re-layouts: 9.49 us -> 2.52 us
    all_gather x6 -> x0, waiting for transfers between devices: 306 us -> none  [the longest x3 146 us: prefix(): pieces = jax.tree.map(lambda part: lax.all_gather(part, axis), value)]
    pallas_call x0 -> x1, Pallas kernels: none -> 112 us  [per_device(): pl.pallas_call(functools.partial(kernel, scale), out_shape=(jax.ShapeDtyp...]
    select_n x63 -> x0, other arithmetic: 62.5 us -> none  [the longest x62 62.4 us: hop(): jnp.where(position < mine, new, old)]
    reduce_scatter x1 -> x0, waiting for transfers between devices: 53.7 us -> none  [per_device(): lax.psum_scatter(partial_grad, 'head', scatter_dimension=1, tiled=True)]
    dot_general x19 -> x0, matrix products: 27 us -> none  [the longest x1 6.65 us: per_device(): jnp.einsum('tcj,cdj->td', grad_qkv, policy_whole, preferred_element_type=...]
  transfers between devices with their start and end apart: 7 -> 0, of which waited for: 7 -> 0; matrix products, arithmetic and copies ran while one was open for 5% -> 0% of each run, Pallas kernels for 0% -> 0%
where the time goes in v1:
time: 115 us
  Pallas kernels  112 us (97%)
  local copies, waits for them, and re-layouts  2.52 us (2%)
    pallas_call x1, Pallas kernels, per_device(): pl.pallas_call(functools.partial(kernel, scale), out_shape=(jax.ShapeDtyp...  112 us
    unnamed x4, local copies, waits for them, and re-layouts  2.52 us

profile of v1, /device:TPU:1, one launch (start us, length us, event | category | flops | bytes accessed | tf_op | source)
XLA Modules:
  0.0 114.8 jit_solution(4691532228545583182)
XLA Ops:
  0.6 111.6 %shard_map.50 = (f32[256,256]{1,0:T(8,128)}, f32[256,512]{1,0:T(8,128)}) custom-call(bf16[256,512]{1,0:T(8,128)(2,1)} %tok_ref.1, bf16[3,128,256]{2,1,0:T(8,128)(2,1)} %pol_ref.1, bf16[3,128,256]{2,1,0:T(8,128)(2,1)} %ref_ref.1), custom_call_target="tpu_custom_call" | custom-call | tf_op jit(solution)/shard_map/pallas_call | solution.py:352
  112.2 0.0 copy-start
  112.3 1.7 %copy.7 = f32[256,256]{1,0:T(8,128)} copy(f32[256,256]{1,0:T(8,128)} %get-tuple-element.4) | data formatting | bytes 524288
  114.0 0.0 copy-done
  114.0 0.8 copy.8
Async XLA Ops:
  112.2 1.7 %copy-start = (f32[256,512]{1,0:T(8,128)S(1)}, f32[256,512]{1,0:T(8,128)}, u32[]{:S(2)}) copy-start(f32[256,512]{1,0:T(8,128)} %get-tuple-element.5) | copy-start | bytes 1572868

commit v2 on v1

v2 whole, which is shorter than its diff:
```python
import functools
import math

import jax
import jax.numpy as jnp
from jax import lax
from jax.experimental import pallas as pl
from jax.experimental.pallas import tpu as pltpu
from jax.sharding import PartitionSpec as P

HD = 128
F32 = jnp.float32
BF16 = jnp.bfloat16
MESH = pl.DeviceIdType.MESH

PIECES = ((0, 1), (0, 2), (1, 1), (1, 2), (0, 0), (1, 0))
KP, VP, KR, VR, QP, QR = range(6)


def mm(a, b, ca, cb):
    return lax.dot_general(a, b, (((ca,), (cb,)), ((), ())), preferred_element_type=F32)


def split(a):
    high = a.astype(BF16)
    return high, (a - high.astype(F32)).astype(BF16)


def mm3(a, b, ca, cb):
    return mm(a[0], b[0], ca, cb) + (mm(a[0], b[1], ca, cb) + mm(a[1], b[0], ca, cb))


def kernel(
    scale, tok_ref, pol_ref, ref_ref, diff_ref, grad_ref,
    w, xs, acc, att, sc, g, own_f, sib_f, chip_f, got1_f, msg_f, got2_f, fin_f, got_f, pre_f,
    own_b, sib_b, chip_b, got1_b, msg_b, got2_b, fin_b, got_b, pre_b,
    out_r, in_r, out_l, in_l,
    local_sem, p1_send, p1_recv, p2_send, p2_recv, sib_send, sib_recv,
    tok_send, tok_recv, pre_send, pre_recv, rs_send, rs_recv,
):
    ctx, z = lax.axis_index("ctx"), lax.axis_index("head")
    y, x, k = ctx // 8, lax.rem(ctx // 2, 4), lax.rem(ctx, 2)
    zs = lax.axis_size("head")

    def at(yy, xx, kk):
        return ((yy * 4 + xx) * 2 + kk, z)

    def turn(i, by):
        return lax.rem(i + by + 4, 4)

    xdev = [at(y, turn(x, d), k) for d in range(4)]
    ydev = [at(turn(y, d), x, k) for d in range(4)]
    sibling = at(y, x, 1 - k)
    zr, zl = (ctx, lax.rem(z + 1, zs)), (ctx, lax.rem(z + zs - 1, zs))

    def zb(by):
        return lax.rem(z + by + zs, zs)

    barrier = pltpu.get_barrier_semaphore()
    greeted = xdev[1:] + ydev[1:] + [sibling, zr, zl]
    for dev in greeted:
        pl.semaphore_signal(barrier, inc=1, device_id=dev, device_id_type=MESH)
    pl.semaphore_wait(barrier, len(greeted))

    sent = []

    def send(src, dst, ssem, rsem, dev):
        copy = pltpu.make_async_remote_copy(
            src_ref=src, dst_ref=dst, send_sem=ssem, recv_sem=rsem,
            device_id=dev, device_id_type=MESH,
        )
        copy.start()
        sent.append(copy)

    def arrived(dst, sem):
        pltpu.make_async_remote_copy(
            src_ref=dst, dst_ref=dst, send_sem=sem, recv_sem=sem,
            device_id=sibling, device_id_type=MESH,
        ).wait_recv()

    def source(s):
        model, slot = PIECES[s]
        return (pol_ref, ref_ref)[model].at[slot]

    def block(s, i, j):
        return w.at[s, j, i, k] if s % 2 == 0 else w.at[s, i, j, k]

    def part(s, i, j, half):
        rows = pl.ds(64 * half, 64)
        return w.at[s, j, i, k, rows] if s % 2 == 0 else w.at[s, i, j, k, rows]

    def group(s, j, kk):
        return w.at[s, j, :, kk] if s % 2 == 0 else w.at[s, :, j, kk]

    def some(s, j, half, kk):
        few = pl.ds(2 * half, 2)
        return w.at[s, j, few, kk] if s % 2 == 0 else w.at[s, few, j, kk]

    def axes(s):
        return (x, y, xdev, ydev) if s % 2 == 0 else (y, x, ydev, xdev)

    def pair(stage):
        return (2 * stage, 2 * stage + 1)

    def p1_start(stage):
        for s in pair(stage):
            i, j, first, _ = axes(s)
            for n, d in ((0, 1), (1, 3)):
                send(source(s), block(s, i, j), p1_send.at[s, n], p1_recv.at[s, n], first[d])

    def p1_forward(stage):
        for n, d, to in ((0, -1, 1), (1, 1, 3)):
            for s in pair(stage):
                i, j, first, _ = axes(s)
                arrived(block(s, turn(i, d), j), p1_recv.at[s, n])
                half = part(s, turn(i, d), j, n)
                send(half, half, p1_send.at[s, 2 + n], p1_recv.at[s, 2 + n], first[to])

    def p1_done(stage):
        for s in pair(stage):
            i, j, _, _ = axes(s)
            for n in range(2):
                arrived(part(s, turn(i, 2), j, n), p1_recv.at[s, 2 + n])

    def p2_start(stage):
        for later_half in range(2):
            for s in pair(stage):
                _, j, _, second = axes(s)
                for n, d in ((0, 1), (1, 3)):
                    mine = some(s, j, n ^ later_half, k)
                    at_n = 2 * n + later_half
                    send(mine, mine, p2_send.at[s, at_n], p2_recv.at[s, at_n], second[d])

    def sib_start(stage):
        for s in pair(stage):
            mine = group(s, axes(s)[1], k)
            send(mine, mine, sib_send.at[s, 0], sib_recv.at[s, 0], sibling)

    def p2_forward(stage):
        for n, d, to in ((0, -1, 1), (1, 1, 3)):
            for s in pair(stage):
                _, j, _, second = axes(s)
                half = some(s, turn(j, d), n, k)
                arrived(half, p2_recv.at[s, 2 * n])
                send(half, half, p2_send.at[s, 4 + n], p2_recv.at[s, 4 + n], second[to])

    def p2_sides(stage):
        for n, d in ((0, -1), (1, 1)):
            for s in pair(stage):
                j = axes(s)[1]
                arrived(some(s, turn(j, d), 1 - n, k), p2_recv.at[s, 2 * n + 1])
                theirs = group(s, turn(j, d), k)
                send(theirs, theirs, sib_send.at[s, 1 + n], sib_recv.at[s, 1 + n], sibling)

    def p2_done(stage):
        for n in range(2):
            for s in pair(stage):
                half = some(s, turn(axes(s)[1], 2), n, k)
                arrived(half, p2_recv.at[s, 4 + n])
                send(half, half, sib_send.at[s, 3 + n], sib_recv.at[s, 3 + n], sibling)

    def sib_sides(stage):
        for s in pair(stage):
            j = axes(s)[1]
            for n, d in ((0, 0), (1, -1), (2, 1)):
                arrived(group(s, turn(j, d), 1 - k), sib_recv.at[s, n])

    def sib_done(stage):
        for s in pair(stage):
            for n in range(2):
                arrived(some(s, turn(axes(s)[1], 2), n, 1 - k), sib_recv.at[s, 3 + n])

    def tok(by, c):
        return xs.at[2 * zb(by) + c]

    def tok_start():
        for c in range(2):
            for n, to in ((0, zr), (1, zl)):
                cc = c ^ n
                src = tok_ref.at[:, pl.ds(256 * cc, 256)]
                send(src, tok(0, cc), tok_send.at[n, 0, cc], tok_recv.at[n, 0, cc], to)

    def tok_forward(step):
        for c in range(2):
            for n, by, to in ((0, -step, zr), (1, step, zl)):
                cc = c ^ n
                arrived(tok(by, cc), tok_recv.at[n, step - 1, cc])
                if step < 3 or c == 0:
                    send(
                        tok(by, cc), tok(by, cc),
                        tok_send.at[n, step, cc], tok_recv.at[n, step, cc], to,
                    )

    def tok_done():
        for n in range(2):
            arrived(tok(4, n), tok_recv.at[n, 3, n])

    def chunk(s, f):
        return w[s, f // 4, lax.rem(f, 4)].reshape(256, 256)

    def add_chunks(s, chunks, first):
        total = acc[s] if not first else None
        for f in chunks:
            value = mm(xs[f], chunk(s, f), 1, 0)
            total = value if total is None else total + value
        acc[s] = total

    def project_tokens(stage, places, first=False):
        for s in pair(stage):
            add_chunks(s, [2 * zb(by) + c for by in places for c in range(2)], first)

    def project_group(stage, d, first=False):
        for s in pair(stage):
            j = turn(axes(s)[1], d)
            add_chunks(s, [4 * j + i if s % 2 == 0 else 4 * i + j for i in range(4)], first)

    def head(s, hh):
        return acc[s, :, hh * HD:(hh + 1) * HD]

    up, low = pl.ds(0, 64), pl.ds(64, 64)

    def rows_in(ref, lead, few):
        inner = len(ref.shape) - len(lead) - 2
        return ref.at[(*lead, *[slice(None)] * inner, few)]

    def sum_start(t, own, sib):
        send(own.at[1 - k], sib, pre_send.at[t, 0], pre_recv.at[t, 0], sibling)

    def sum_one(t, own, sib, chip, got1):
        arrived(sib, pre_recv.at[t, 0])
        chip[...] = own[k] + sib[...]
        for d in (2, 1, 3):
            for q, devs, i, few in ((0, xdev, x, up), (1, ydev, y, low)):
                at_n = 3 * q + d
                send(
                    rows_in(chip, (), few), got1.at[q, i],
                    pre_send.at[t, at_n], pre_recv.at[t, at_n], devs[d],
                )

    def sum_two(t, chip, got1, msg, got2, pre, before):
        total = rows_in(chip, (), up)[...]
        partial = jnp.zeros_like(total)
        ahead = jnp.zeros_like(total)
        for d in (1, 3, 2):
            at_x, at_y = turn(x, -d), turn(y, -d)
            arrived(got1.at[0, at_x], pre_recv.at[t, d])
            value = got1[0, at_x]
            total += value
            partial += jnp.where(before(at_x, x), value, 0.0)
            arrived(got1.at[1, at_y], pre_recv.at[t, 3 + d])
            ahead += jnp.where(before(at_y, y), got1[1, at_y], 0.0)
        msg[0] = total
        msg[1] = ahead
        msg[2] = ahead + rows_in(chip, (), low)[...]
        rows_in(pre, (), up)[...] = partial
        rows_in(pre, (), low)[...] = ahead
        for d in (2, 1, 3):
            send(
                msg.at[0], got2.at[0, y],
                pre_send.at[t, 6 + d], pre_recv.at[t, 6 + d], ydev[d],
            )
            which = jnp.where(before(x, turn(x, d)), 2, 1)
            send(
                msg.at[which], got2.at[1, x],
                pre_send.at[t, 9 + d], pre_recv.at[t, 9 + d], xdev[d],
            )

    def sum_three(t, own, sib, got2, fin, got, pre, before, last):
        upper, lower = rows_in(pre, (), up)[...], rows_in(pre, (), low)[...]
        for d in (1, 3, 2):
            at_x, at_y = turn(x, -d), turn(y, -d)
            arrived(got2.at[0, at_y], pre_recv.at[t, 6 + d])
            upper += jnp.where(before(at_y, y), got2[0, at_y], 0.0)
            arrived(got2.at[1, at_x], pre_recv.at[t, 9 + d])
            lower += got2[1, at_x]
        rows_in(pre, (), up)[...] = upper
        rows_in(pre, (), low)[...] = lower
        total = pre[...]
        fin[...] = total + jnp.where(k != last, own[k], 0.0)
        send(fin, got, pre_send.at[t, 13], pre_recv.at[t, 13], sibling)
        pre[...] = total + jnp.where(k == last, sib[...], 0.0)

    def sum_four(t, got):
        arrived(got, pre_recv.at[t, 13])

    earlier = lambda a, b: a < b
    later = lambda a, b: a > b

    def copies():
        yield from (
            pltpu.make_async_copy(source(s), w.at[s, y, x, k], local_sem.at[s])
            for s in range(6)
        )
        yield from (
            pltpu.make_async_copy(
                tok_ref.at[:, pl.ds(256 * c, 256)], tok(0, c), local_sem.at[6 + c]
            )
            for c in range(2)
        )

    for stage in range(3):
        p1_start(stage)
    tok_start()
    for copy in copies():
        copy.start()
    for copy in copies():
        copy.wait()
    for stage in range(3):
        p1_forward(stage)
    p1_done(0)
    p2_start(0)
    sib_start(0)
    p1_done(1)
    p1_done(2)
    tok_forward(1)
    p2_forward(0)
    p2_start(1)
    sib_start(1)
    tok_forward(2)
    p2_sides(0)
    p2_done(0)
    tok_forward(3)
    sib_sides(0)
    sib_done(0)
    project_tokens(0, (0, -1), True)
    p2_forward(1)
    p2_start(2)
    sib_start(2)
    project_tokens(0, (1, -2))
    project_tokens(0, (2, -3))
    p2_sides(1)
    tok_done()
    project_tokens(0, (3, 4))
    for hh in range(2):
        own_f[hh, 0] = mm3(split(head(KP, hh)), split(head(VP, hh)), 0, 0)
    sib_sides(1)
    project_group(1, 0, True)
    p2_done(1)
    project_group(1, -1)
    project_group(1, 1)
    sib_done(1)
    project_group(1, 2)
    for hh in range(2):
        own_f[hh, 1] = mm3(split(head(KR, hh)), split(head(VR, hh)), 0, 0)
    sum_start(0, own_f, sib_f)
    p2_forward(2)
    sum_one(0, own_f, sib_f, chip_f, got1_f)
    p2_sides(2)
    sib_sides(2)
    project_group(2, 0, True)
    project_group(2, -1)
    sum_two(0, chip_f, got1_f, msg_f, got2_f, pre_f, earlier)
    project_group(2, 1)
    p2_done(2)
    sib_done(2)
    project_group(2, 2)

    rows = lax.broadcasted_iota(jnp.int32, (256, 256), 0)
    columns = lax.broadcasted_iota(jnp.int32, (256, 256), 1)
    causal = rows >= columns

    def prefix(model, hh):
        return jnp.where(k == hh, pre_f[model], got_f[model])

    PAIRS = ((QP, KP, VP), (QR, KR, VR))
    for hh in range(2):
        cols = slice(hh * HD, (hh + 1) * HD)
        for model, (qs, ks, vs) in enumerate(PAIRS):
            q, kk, v = (split(head(s, hh)) for s in (qs, ks, vs))
            scores = split(jnp.where(causal, mm3(q, kk, 1, 1), 0.0))
            att[model, :, cols] = mm3(scores, v, 1, 0)
            if model == 0:
                sc[hh, 0], sc[hh, 1] = scores
    sum_three(0, own_f, sib_f, got2_f, fin_f, got_f, pre_f, earlier, 1)
    sum_four(0, got_f)
    for hh in range(2):
        cols = slice(hh * HD, (hh + 1) * HD)
        outs = [
            scale * (att[m, :, cols] + mm3(split(head(qs, hh)), split(prefix(m, hh)), 1, 0))
            for m, qs in enumerate((QP, QR))
        ]
        diff = outs[0] - outs[1]
        diff_ref[:, cols] = diff
        own_b[hh] = mm3(split(head(QP, hh)), split(diff), 0, 0)
    sum_start(1, own_b, sib_b)
    sum_one(1, own_b, sib_b, chip_b, got1_b)

    for hh in range(2):
        cols = slice(hh * HD, (hh + 1) * HD)
        q, kk, v = (split(head(s, hh)) for s in (QP, KP, VP))
        diff = split(diff_ref[:, cols])
        weighted = split(jnp.where(causal, mm3(diff, v, 1, 1), 0.0))
        dq = mm3(weighted, kk, 1, 0) + mm3(diff, split(prefix(0, hh)), 1, 1)
        g[0, :, cols] = (scale * dq).astype(BF16)
        att[0, :, cols] = mm3(weighted, q, 0, 0)
        att[1, :, cols] = mm3((sc[hh, 0], sc[hh, 1]), diff, 0, 0)
        if hh == 0:
            sum_two(1, chip_b, got1_b, msg_b, got2_b, pre_b, later)
    sum_three(1, own_b, sib_b, got2_b, fin_b, got_b, pre_b, later, 0)
    sum_four(1, got_b)
    for hh in range(2):
        cols = slice(hh * HD, (hh + 1) * HD)
        kk, v = (split(head(s, hh)) for s in (KP, VP))
        suffix = split(jnp.where(k == hh, pre_b[...], got_b[...]))
        g[1, :, cols] = (scale * (att[0, :, cols] + mm3(v, suffix, 1, 1))).astype(BF16)
        g[2, :, cols] = (scale * (att[1, :, cols] + mm3(kk, suffix, 1, 0))).astype(BF16)

    def rows_of(s, h):
        return w[s, h // 2, pl.ds(2 * lax.rem(h, 2), 2)].reshape(512, 256)

    def term(by, half):
        h, few = zb(by), slice(128 * half, 128 * half + 128)
        return (
            mm(g[0, few], rows_of(QP, h), 1, 1)
            + mm(g[1, few], rows_of(KP, h), 1, 1)
            + mm(g[2, few], rows_of(VP, h), 1, 1)
        )

    def hop(n, sign, out, inn, to, step, half):
        value = term(sign * (5 - step), half)
        fresh = step == 1 or (step == 2 and half != n)
        if not fresh:
            arrived(inn.at[step - 2, half], rs_recv.at[n, step - 2, half])
            value = value + inn[step - 2, half].astype(F32)
        out[step - 1, half] = value.astype(BF16)
        send(
            out.at[step - 1, half], inn.at[step - 1, half],
            rs_send.at[n, step - 1, half], rs_recv.at[n, step - 1, half], to,
        )

    ways = ((0, 1, out_r, in_r, zr), (1, -1, out_l, in_l, zl))
    for step in range(1, 5):
        for turn_at in range(2):
            for n, sign, out, inn, to in ways:
                half = (1 - n) if turn_at == 0 else n
                if step == 1 and half != n:
                    continue
                hop(n, sign, out, inn, to, step, half)
    for half in range(2):
        few = slice(128 * half, 128 * half + 128)
        grad_ref[few] = term(0, half)
    for turn_at in range(2):
        for n, _, _, inn, _ in ways:
            half = (1 - n) if turn_at == 0 else n
            few = slice(128 * half, 128 * half + 128)
            arrived(inn.at[3, half], rs_recv.at[n, 3, half])
            grad_ref[few] += inn[3, half].astype(F32)
    for copy in sent:
        copy.wait_send()


def per_device(tokens, policy_weight, reference_weight):
    seq = tokens.shape[0] * lax.axis_size("ctx")
    scale = 1.0 / math.sqrt(HD * seq)

    def sums(*models):
        whole = pltpu.VMEM((*models, HD, HD), F32)
        some = lambda *lead: pltpu.VMEM((*lead, *models, HD // 2, HD), F32)
        own = pltpu.VMEM((2, *models, HD, HD), F32)
        return own, whole, whole, some(2, 4), some(3), some(2, 4), whole, whole, whole

    half = pltpu.VMEM((4, 2, 128, 512), BF16)
    dma = pltpu.SemaphoreType.DMA
    return pl.pallas_call(
        functools.partial(kernel, scale),
        out_shape=(
            pltpu.VMEM((256, 256), F32),
            pltpu.VMEM((256, 512), F32),
        ),
        in_specs=[pl.BlockSpec(memory_space=pl.ANY)] * 3,
        out_specs=[pl.BlockSpec(memory_space=pltpu.VMEM)] * 2,
        scratch_shapes=[
            pltpu.VMEM((6, 4, 4, 2, 128, 256), BF16),
            pltpu.VMEM((16, 256, 256), BF16),
            pltpu.VMEM((6, 256, 256), F32),
            pltpu.VMEM((2, 256, 256), F32),
            pltpu.VMEM((2, 2, 256, 256), BF16),
            pltpu.VMEM((3, 256, 256), BF16),
            *sums(2),
            *sums(),
            half, half, half, half,
            dma((8,)), dma((6, 4)), dma((6, 4)), dma((6, 6)), dma((6, 6)), dma((6, 5)),
            dma((6, 5)), dma((2, 4, 2)), dma((2, 4, 2)), dma((2, 14)), dma((2, 14)),
            dma((2, 4, 2)), dma((2, 4, 2)),
        ],
        compiler_params=pltpu.CompilerParams(
            collective_id=0, has_side_effects=True, vmem_limit_bytes=58 * 2**20
        ),
    )(tokens, policy_weight, reference_weight)


def solution(mesh):
    in_specs = (P("ctx", "head"), P(None, "ctx", "head"), P(None, "ctx", "head"))
    out_specs = (P("ctx", "head"), P("ctx", "head"))
    return jax.shard_map(
        per_device, mesh=mesh, in_specs=in_specs, out_specs=out_specs, check_vma=False
    )
```

time: 115 us -> 95.4 us (0.83)
  Pallas kernels: 112 us -> 93.1 us
    pallas_call x1, Pallas kernels: 112 us -> 93.1 us  [per_device(): pl.pallas_call(functools.partial(kernel, scale), out_shape=(pltpu.VMEM((2...]
    unnamed x4 -> x2, local copies, waits for them, and re-layouts: 2.52 us -> 1.5 us
where the time goes in v2:
time: 95.4 us; the launch traced here: 95.3 us
  Pallas kernels  93.1 us (98%)
  local copies, waits for them, and re-layouts  1.5 us (2%)
    pallas_call x1, Pallas kernels, per_device(): pl.pallas_call(functools.partial(kernel, scale), out_shape=(pltpu.VMEM((2...  93.1 us

profile of v2, /device:TPU:1, one launch (start us, length us, event | category | flops | bytes accessed | tf_op | source)
XLA Modules:
  0.0 95.3 jit_solution(13818873668238787025)
XLA Ops:
  0.6 93.1 %shard_map.50 = (f32[256,256]{1,0:T(8,128)S(1)}, f32[256,512]{1,0:T(8,128)S(1)}) custom-call(bf16[256,512]{1,0:T(8,128)(2,1)} %tok_ref.1, bf16[3,128,256]{2,1,0:T(8,128)(2,1)} %pol_ref.1, bf16[3,128,256]{2,1,0:T(8,128)(2,1)} %ref_ref.1), custom_call_target="tpu_custom_call" | custom-call | tf_op jit(solution)/shard_map/pallas_call | solution.py:464
  93.8 0.7 copy.7
  94.5 0.8 copy.8

commit v3 on v2

v3 whole, which is shorter than its diff:
```python
import functools
import math

import jax
import jax.numpy as jnp
from jax import lax
from jax.experimental import pallas as pl
from jax.experimental.pallas import tpu as pltpu
from jax.sharding import PartitionSpec as P

HD = 128
F32 = jnp.float32
BF16 = jnp.bfloat16
MESH = pl.DeviceIdType.MESH

PIECES = ((0, 1), (0, 2), (1, 1), (1, 2), (0, 0), (1, 0))
KP, VP, KR, VR, QP, QR = range(6)


def mm(a, b, ca, cb):
    return lax.dot_general(a, b, (((ca,), (cb,)), ((), ())), preferred_element_type=F32)


def split(a):
    high = a.astype(BF16)
    return high, (a - high.astype(F32)).astype(BF16)


def mm3(a, b, ca, cb):
    return mm(a[0], b[0], ca, cb) + (mm(a[0], b[1], ca, cb) + mm(a[1], b[0], ca, cb))


def kernel(
    scale, tok_ref, pol_ref, ref_ref, diff_ref, grad_ref,
    w, w2, xs, acc, att, sc, ed, dgot, g, gx, sums,
    out_r, in_r, out_l, in_l,
    local_sem, give_send, give_recv, p1_send, p1_recv, p2_send, p2_recv, sib_send, sib_recv,
    tok_send, tok_recv, pre_send, pre_recv, rs_send, rs_recv,
):
    ctx, z = lax.axis_index("ctx"), lax.axis_index("head")
    y, x, k = ctx // 8, lax.rem(ctx // 2, 4), lax.rem(ctx, 2)
    zs = lax.axis_size("head")

    def at(yy, xx, kk):
        return ((yy * 4 + xx) * 2 + kk, z)

    def turn(i, by):
        return lax.rem(i + by + 4, 4)

    xdev = [at(y, turn(x, d), k) for d in range(4)]
    ydev = [at(turn(y, d), x, k) for d in range(4)]
    sibling = at(y, x, 1 - k)
    zr, zl = (ctx, lax.rem(z + 1, zs)), (ctx, lax.rem(z + zs - 1, zs))

    def zb(by):
        return lax.rem(z + by + zs, zs)

    barrier = pltpu.get_barrier_semaphore()
    greeted = xdev[1:] + ydev[1:] + [sibling, zr, zl]
    for dev in greeted:
        pl.semaphore_signal(barrier, inc=1, device_id=dev, device_id_type=MESH)
    pl.semaphore_wait(barrier, len(greeted))

    sent = []

    def send(src, dst, ssem, rsem, dev):
        copy = pltpu.make_async_remote_copy(
            src_ref=src, dst_ref=dst, send_sem=ssem, recv_sem=rsem,
            device_id=dev, device_id_type=MESH,
        )
        copy.start()
        sent.append(copy)

    def arrived(dst, sem):
        pltpu.make_async_remote_copy(
            src_ref=dst, dst_ref=dst, send_sem=sem, recv_sem=sem,
            device_id=sibling, device_id_type=MESH,
        ).wait_recv()

    def lanes(kk):
        return pl.ds(pl.multiple_of(HD * kk, HD), HD)

    def half_rows(p):
        return pl.ds(pl.multiple_of(128 * p, 128), 128)

    def core_rows(kk):
        return pl.ds(pl.multiple_of(256 * kk, 256), 256)

    def source(s, kk):
        model, slot = PIECES[s]
        return (pol_ref, ref_ref)[model].at[slot, :, lanes(kk)]

    def block(s, i, j):
        return w.at[s, j, i] if s % 2 == 0 else w.at[s, i, j]

    def part(s, i, j, p):
        rows = half_rows(p)
        return w.at[s, j, i, rows] if s % 2 == 0 else w.at[s, i, j, rows]

    def some(s, j, half):
        few = pl.ds(2 * half, 2)
        return w.at[s, j, few] if s % 2 == 0 else w.at[s, few, j]

    def axes(s):
        return (x, y, xdev, ydev) if s % 2 == 0 else (y, x, ydev, xdev)

    def pair(stage):
        return (2 * stage, 2 * stage + 1)

    def give(stage):
        for s in pair(stage):
            send(
                source(s, 1 - k), w.at[s, y, x, half_rows(k)],
                give_send.at[s], give_recv.at[s], sibling,
            )

    def p1_start(stage):
        for s in pair(stage):
            i, j, first, _ = axes(s)
            for n, d in ((0, 1), (1, 3)):
                at_n = 2 * n + k
                send(
                    source(s, k), part(s, i, j, k),
                    p1_send.at[s, at_n], p1_recv.at[s, at_n], first[d],
                )

    def p1_given(stage):
        for s in pair(stage):
            i, j, first, _ = axes(s)
            given = part(s, i, j, 1 - k)
            arrived(given, give_recv.at[s])
            for n, d in ((0, 1), (1, 3)):
                at_n = 2 * n + 1 - k
                send(given, given, p1_send.at[s, at_n], p1_recv.at[s, at_n], first[d])

    def p1_forward(stage):
        for n, d, to in ((0, -1, 1), (1, 1, 3)):
            for s in pair(stage):
                i, j, first, _ = axes(s)
                half = part(s, turn(i, d), j, n)
                arrived(half, p1_recv.at[s, 3 * n])
                send(half, half, p1_send.at[s, 4 + n], p1_recv.at[s, 4 + n], first[to])

    def p1_done(stage):
        for s in pair(stage):
            i, j, _, _ = axes(s)
            for n, d in ((0, -1), (1, 1)):
                arrived(part(s, turn(i, d), j, 1 - n), p1_recv.at[s, 1 + n])
            for n in range(2):
                arrived(part(s, turn(i, 2), j, n), p1_recv.at[s, 4 + n])

    def p2_start(stage, second_half):
        for s in pair(stage):
            _, j, _, second = axes(s)
            for n, d in ((0, 1), (1, 3)):
                mine = some(s, j, n ^ second_half)
                at_n = 2 * n + second_half
                send(mine, mine, p2_send.at[s, at_n], p2_recv.at[s, at_n], second[d])

    def p2_forward(stage):
        for n, d, to in ((0, -1, 1), (1, 1, 3)):
            for s in pair(stage):
                _, j, _, second = axes(s)
                half = some(s, turn(j, d), n)
                arrived(half, p2_recv.at[s, 2 * n])
                send(half, half, p2_send.at[s, 4 + n], p2_recv.at[s, 4 + n], second[to])

    def p2_sides(stage):
        for n, d in ((0, -1), (1, 1)):
            for s in pair(stage):
                arrived(some(s, turn(axes(s)[1], d), 1 - n), p2_recv.at[s, 2 * n + 1])

    def p2_done(stage):
        for n in range(2):
            for s in pair(stage):
                arrived(some(s, turn(axes(s)[1], 2), n), p2_recv.at[s, 4 + n])

    def share(s, at_n):
        send(w.at[s], w2.at[at_n], sib_send.at[at_n], sib_recv.at[at_n], sibling)

    def tok(by, c):
        return xs.at[2 * zb(by) + c, core_rows(k)]

    def tok_both(by, kk):
        return xs.at[pl.ds(2 * zb(by), 2), core_rows(kk)]

    def tok_share(by, at_n):
        mine = tok_both(by, k)
        send(mine, mine, sib_send.at[at_n], sib_recv.at[at_n], sibling)

    def tok_shared(by, at_n):
        arrived(tok_both(by, 1 - k), sib_recv.at[at_n])

    def tok_start():
        for c in range(2):
            for n, to in ((0, zr), (1, zl)):
                cc = c ^ n
                src = tok_ref.at[:, pl.ds(256 * cc, 256)]
                send(src, tok(0, cc), tok_send.at[n, 0, cc], tok_recv.at[n, 0, cc], to)

    def tok_forward(step):
        for c in range(2):
            for n, by, to in ((0, -step, zr), (1, step, zl)):
                cc = c ^ n
                arrived(tok(by, cc), tok_recv.at[n, step - 1, cc])
                if step < 3 or c == 0:
                    send(
                        tok(by, cc), tok(by, cc),
                        tok_send.at[n, step, cc], tok_recv.at[n, step, cc], to,
                    )
        tok_share(-step, 3 + 2 * step)
        tok_share(step, 4 + 2 * step)

    def tok_done():
        for n in range(2):
            arrived(tok(4, n), tok_recv.at[n, 3, n])
        tok_share(4, 4)

    def both(ref, first, second, f):
        at_f = (f // 4, lax.rem(f, 4))
        return jnp.concatenate([ref[first, *at_f], ref[second, *at_f]], 1)

    def add_chunks(stage, chunks, first):
        total = acc[stage] if not first else None
        for f in chunks:
            value = mm(xs[f], both(w, *pair(stage), f), 1, 0)
            total = value if total is None else total + value
        acc[stage] = total

    def project_tokens(stage, places, first=False):
        add_chunks(stage, [2 * zb(by) + c for by in places for c in range(2)], first)

    def project_rows(stage, yy, first=False):
        add_chunks(stage, [4 * yy + i for i in range(4)], first)

    def project_apart(stage, d, first=False):
        for s in pair(stage):
            j = turn(axes(s)[1], d)
            cols = slice(HD * (s % 2), HD * (s % 2) + HD)
            total = acc[stage, :, cols] if not first else None
            for i in range(4):
                at_f = (j, i) if s % 2 == 0 else (i, j)
                value = mm(xs[4 * at_f[0] + at_f[1]], w[s, *at_f], 1, 0)
                total = value if total is None else total + value
            acc[stage, :, cols] = total

    def piece(s):
        return acc[s // 2, :, (s % 2) * HD:(s % 2 + 1) * HD]

    up, low = pl.ds(0, 64), pl.ds(64, 64)

    def sum_one(t):
        chip, got1 = sums[t][:2]
        for d in (2, 1, 3):
            for q, devs, i, few in ((0, xdev, x, up), (1, ydev, y, low)):
                at_n = 3 * q + d - 1
                send(
                    chip.at[few], got1.at[q, i],
                    pre_send.at[t, at_n], pre_recv.at[t, at_n], devs[d],
                )

    def sum_two(t, before):
        chip, got1, msg, got2, pre = sums[t]
        total = chip[:64]
        partial = jnp.zeros_like(total)
        ahead = jnp.zeros_like(total)
        for d in (1, 3, 2):
            at_x, at_y = turn(x, -d), turn(y, -d)
            arrived(got1.at[0, at_x], pre_recv.at[t, d - 1])
            value = got1[0, at_x]
            total += value
            partial += jnp.where(before(at_x, x), value, 0.0)
            arrived(got1.at[1, at_y], pre_recv.at[t, 2 + d])
            ahead += jnp.where(before(at_y, y), got1[1, at_y], 0.0)
        msg[0] = total
        msg[1] = ahead
        msg[2] = ahead + chip[64:]
        for d in (2, 1, 3):
            send(
                msg.at[0], got2.at[0, y],
                pre_send.at[t, 5 + d], pre_recv.at[t, 5 + d], ydev[d],
            )
            which = jnp.where(before(x, turn(x, d)), 2, 1)
            send(
                msg.at[which], got2.at[1, x],
                pre_send.at[t, 8 + d], pre_recv.at[t, 8 + d], xdev[d],
            )
        pre[:64] = partial
        pre[64:] = ahead

    def sum_three(t, before):
        _, _, _, got2, pre = sums[t]
        upper, lower = pre[:64], pre[64:]
        for d in (1, 3, 2):
            at_x, at_y = turn(x, -d), turn(y, -d)
            arrived(got2.at[0, at_y], pre_recv.at[t, 5 + d])
            upper += jnp.where(before(at_y, y), got2[0, at_y], 0.0)
            arrived(got2.at[1, at_x], pre_recv.at[t, 8 + d])
            lower += got2[1, at_x]
        pre[:64] = upper
        pre[64:] = lower

    def result(t):
        return split(sums[t][4][...])

    def cut(a, rows):
        return a[0][rows], a[1][rows]

    earlier = lambda a, b: a < b
    later = lambda a, b: a > b

    def copies():
        yield from (
            pltpu.make_async_copy(source(s, k), w.at[s, y, x, half_rows(k)], local_sem.at[s])
            for s in range(6)
        )
        yield from (
            pltpu.make_async_copy(
                tok_ref.at[:, pl.ds(256 * c, 256)], tok(0, c), local_sem.at[6 + c]
            )
            for c in range(2)
        )

    for stage in range(3):
        give(stage)
    p1_start(0)
    p1_start(1)
    tok_start()
    p1_given(0)
    p1_given(1)
    p1_start(2)
    p1_given(2)
    for copy in copies():
        copy.start()
    for copy in copies():
        copy.wait()
    tok_share(0, 3)
    for stage in range(3):
        p1_forward(stage)
    p1_done(0)
    p2_start(0, 0)
    p2_start(0, 1)
    p1_done(1)
    p1_done(2)
    tok_forward(1)
    p2_forward(0)
    p2_start(1, 0)
    p2_start(1, 1)
    tok_forward(2)
    p2_sides(0)
    p2_done(0)
    tok_forward(3)
    tok_shared(0, 3)
    project_tokens(0, (0,), True)
    tok_shared(-1, 5)
    tok_shared(1, 6)
    project_tokens(0, (-1,))
    p2_forward(1)
    p2_start(2, 0)
    project_tokens(0, (1,))
    tok_shared(-2, 7)
    tok_shared(2, 8)
    project_tokens(0, (-2, 2))
    tok_done()
    tok_shared(-3, 9)
    tok_shared(3, 10)
    project_tokens(0, (-3, 3))
    tok_shared(4, 4)
    project_tokens(0, (4,))
    sums[0][0][...] = mm3(split(piece(KP)), split(piece(VP)), 0, 0)
    sum_one(0)
    p2_start(2, 1)
    p2_sides(1)
    project_apart(1, 0, True)
    project_apart(1, -1)
    project_apart(1, 1)
    p2_done(1)
    project_apart(1, 2)
    sums[1][0][...] = mm3(split(piece(KR)), split(piece(VR)), 0, 0)
    sum_one(1)
    p2_forward(2)
    share(KP, 0)
    share(VP, 1)
    sum_two(0, earlier)
    project_apart(2, 0, True)
    p2_sides(2)
    sum_two(1, earlier)
    project_apart(2, -1)
    project_apart(2, 1)
    p2_done(2)
    project_apart(2, 2)
    share(QP, 2)

    def causal(b):
        shape = (256, 256 * (b + 1))
        rows = lax.broadcasted_iota(jnp.int32, shape, 0) + 256 * b
        return rows >= lax.broadcasted_iota(jnp.int32, shape, 1)

    for model, (qs, ks, vs) in enumerate(((QP, KP, VP), (QR, KR, VR))):
        q, kk, v = (split(piece(s)) for s in (qs, ks, vs))
        for b in range(2):
            mine, upto = slice(256 * b, 256 * b + 256), slice(0, 256 * b + 256)
            scores = mm3(cut(q, mine), cut(kk, upto), 1, 1)
            scores = split(jnp.where(causal(b), scores, 0.0))
            att[model, mine] = mm3(scores, cut(v, upto), 1, 0)
            if model == 0:
                sc[b, 0, :, upto], sc[b, 1, :, upto] = scores
    sum_three(0, earlier)
    att[0] += mm3(split(piece(QP)), result(0), 1, 0)
    sum_three(1, earlier)
    att[1] += mm3(split(piece(QR)), result(1), 1, 0)
    ed[...] = scale * att[0] - scale * att[1]
    sums[2][0][...] = mm3(split(piece(QP)), split(ed[...]), 0, 0)
    sum_one(2)
    theirs = ed.at[core_rows(1 - k)]
    send(theirs, dgot, sib_send.at[11], sib_recv.at[11], sibling)
    diff_ref[:, lanes(k)] = ed[core_rows(k)]

    q, kk, v, e = (split(a) for a in (piece(QP), piece(KP), piece(VP), ed[...]))
    for b in range(2):
        mine, upto = slice(256 * b, 256 * b + 256), slice(0, 256 * b + 256)
        weighted = mm3(cut(e, mine), cut(v, upto), 1, 1)
        weighted = split(jnp.where(causal(b), weighted, 0.0))
        scores = sc[b, 0, :, upto], sc[b, 1, :, upto]
        dq = mm3(weighted, cut(kk, upto), 1, 0) + mm3(cut(e, mine), result(0), 1, 1)
        g[0, mine] = (scale * dq).astype(BF16)
        dk = mm3(weighted, cut(q, mine), 0, 0)
        dv = mm3(scores, cut(e, mine), 0, 0)
        if b == 0:
            att[0, upto], att[1, upto] = dk, dv
            att[0, 256:], att[1, 256:] = jnp.zeros((2, 256, HD), F32)
            sum_two(2, later)
        else:
            att[0, upto] += dk
            att[1, upto] += dv
    send(g.at[0, core_rows(1 - k)], gx.at[0], sib_send.at[12], sib_recv.at[12], sibling)
    for at_n in range(3):
        arrived(w2.at[at_n], sib_recv.at[at_n])
    sum_three(2, later)
    suffix = result(2)
    g[1] = (scale * (att[0] + mm3(split(piece(VP)), suffix, 1, 1))).astype(BF16)
    g[2] = (scale * (att[1] + mm3(split(piece(KP)), suffix, 1, 0))).astype(BF16)
    theirs = g.at[pl.ds(1, 2), core_rows(1 - k)]
    send(theirs, gx.at[pl.ds(1, 2)], sib_send.at[13], sib_recv.at[13], sibling)
    arrived(gx.at[0], sib_recv.at[12])
    arrived(gx.at[pl.ds(1, 2)], sib_recv.at[13])

    def term(by, half):
        h, few = zb(by), slice(128 * half, 128 * half + 128)
        own = pl.ds(pl.multiple_of(256 * k + 128 * half, 128), 128)
        at_h = (h // 2, pl.ds(2 * lax.rem(h, 2), 2))

        def beside(left, right):
            return jnp.concatenate([left, right], 1)

        def rows_of(ref, at_s):
            return ref[at_s, *at_h].reshape(512, HD)

        return (
            mm(beside(g[1, own], g[2, own]), beside(rows_of(w, KP), rows_of(w, VP)), 1, 1)
            + mm(beside(gx[1, few], gx[2, few]), beside(rows_of(w2, 0), rows_of(w2, 1)), 1, 1)
            + mm(beside(g[0, own], gx[0, few]), beside(rows_of(w, QP), rows_of(w2, 2)), 1, 1)
        )

    def hop(n, sign, out, inn, to, step, half):
        value = term(sign * (5 - step), half)
        fresh = step == 1 or (step == 2 and half != n)
        if not fresh:
            arrived(inn.at[step - 2, half], rs_recv.at[n, step - 2, half])
            value = value + inn[step - 2, half].astype(F32)
        out[step - 1, half] = value.astype(BF16)
        send(
            out.at[step - 1, half], inn.at[step - 1, half],
            rs_send.at[n, step - 1, half], rs_recv.at[n, step - 1, half], to,
        )

    ways = ((0, 1, out_r, in_r, zr), (1, -1, out_l, in_l, zl))
    for step in range(1, 5):
        for turn_at in range(2):
            for n, sign, out, inn, to in ways:
                half = (1 - n) if turn_at == 0 else n
                if step == 1 and half != n:
                    continue
                hop(n, sign, out, inn, to, step, half)
    for half in range(2):
        few = slice(128 * half, 128 * half + 128)
        grad_ref[few] = term(0, half)
    for turn_at in range(2):
        for n, _, _, inn, _ in ways:
            half = (1 - n) if turn_at == 0 else n
            few = slice(128 * half, 128 * half + 128)
            arrived(inn.at[3, half], rs_recv.at[n, 3, half])
            grad_ref[few] += inn[3, half].astype(F32)
    arrived(dgot, sib_recv.at[11])
    diff_ref[:, lanes(1 - k)] = dgot[...]
    for copy in sent:
        copy.wait_send()


def per_device(tokens, policy_weight, reference_weight):
    seq = tokens.shape[0] * lax.axis_size("ctx")
    scale = 1.0 / math.sqrt(HD * seq)

    whole = pltpu.VMEM((HD, HD), F32)
    some = lambda *lead: pltpu.VMEM((*lead, HD // 2, HD), F32)
    sums = (whole, some(2, 4), some(3), some(2, 4), whole)
    half = pltpu.VMEM((4, 2, 128, 512), BF16)
    dma = pltpu.SemaphoreType.DMA
    return pl.pallas_call(
        functools.partial(kernel, scale),
        out_shape=(
            pltpu.VMEM((256, 256), F32),
            pltpu.VMEM((256, 512), F32),
        ),
        in_specs=[pl.BlockSpec(memory_space=pl.ANY)] * 3,
        out_specs=[pl.BlockSpec(memory_space=pltpu.VMEM)] * 2,
        scratch_shapes=[
            pltpu.VMEM((6, 4, 4, 256, HD), BF16),
            pltpu.VMEM((3, 4, 4, 256, HD), BF16),
            pltpu.VMEM((16, 512, 256), BF16),
            pltpu.VMEM((3, 512, 2 * HD), F32),
            pltpu.VMEM((2, 512, HD), F32),
            pltpu.VMEM((2, 2, 256, 512), BF16),
            pltpu.VMEM((512, HD), F32),
            pltpu.VMEM((256, HD), F32),
            pltpu.VMEM((3, 512, HD), BF16),
            pltpu.VMEM((3, 256, HD), BF16),
            (sums, sums, sums),
            half, half, half, half,
            dma((8,)), dma((6,)), dma((6,)), dma((6, 6)), dma((6, 6)), dma((6, 6)), dma((6, 6)),
            dma((14,)), dma((14,)), dma((2, 4, 2)), dma((2, 4, 2)), dma((3, 12)), dma((3, 12)),
            dma((2, 4, 2)), dma((2, 4, 2)),
        ],
        compiler_params=pltpu.CompilerParams(
            collective_id=0, has_side_effects=True, vmem_limit_bytes=58 * 2**20
        ),
    )(tokens, policy_weight, reference_weight)


def solution(mesh):
    in_specs = (P("ctx", "head"), P(None, "ctx", "head"), P(None, "ctx", "head"))
    out_specs = (P("ctx", "head"), P("ctx", "head"))
    return jax.shard_map(
        per_device, mesh=mesh, in_specs=in_specs, out_specs=out_specs, check_vma=False
    )
```

time: 95.4 us -> 92.2 us (0.966)
  Pallas kernels: 93.1 us -> 90 us
    pallas_call x1, Pallas kernels: 93.1 us -> 90 us  [per_device(): pl.pallas_call(functools.partial(kernel, scale), out_shape=(pltpu.VMEM((2...]
where the time goes in v3:
time: 92.2 us; the launch traced here: 92.1 us
  Pallas kernels  90 us (98%)
  local copies, waits for them, and re-layouts  1.5 us (2%)
    pallas_call x1, Pallas kernels, per_device(): pl.pallas_call(functools.partial(kernel, scale), out_shape=(pltpu.VMEM((2...  90 us

profile of v3, /device:TPU:1, one launch (start us, length us, event | category | flops | bytes accessed | tf_op | source)
XLA Modules:
  0.0 92.1 jit_solution(5560165351159997869)
XLA Ops:
  0.6 90.0 %shard_map.50 = (f32[256,256]{1,0:T(8,128)S(1)}, f32[256,512]{1,0:T(8,128)S(1)}) custom-call(bf16[256,512]{1,0:T(8,128)(2,1)} %tok_ref.1, bf16[3,128,256]{2,1,0:T(8,128)(2,1)} %pol_ref.1, bf16[3,128,256]{2,1,0:T(8,128)(2,1)} %ref_ref.1), custom_call_target="tpu_custom_call" | custom-call | tf_op jit(solution)/shard_map/pallas_call | solution.py:509
  90.6 0.7 copy.7
  91.3 0.8 copy.8

commit v4 on v3

--- a/solution.py
+++ b/solution.py
@@ -32,7 +32,7 @@
 
 def kernel(
     scale, tok_ref, pol_ref, ref_ref, diff_ref, grad_ref,
-    w, w2, xs, acc, att, sc, ed, dgot, g, gx, sums,
+    w, w2, given_away, xs, acc, att, sc, ed, dgot, g, gx, sums,
     out_r, in_r, out_l, in_l,
     local_sem, give_send, give_recv, p1_send, p1_recv, p2_send, p2_recv, sib_send, sib_recv,
     tok_send, tok_recv, pre_send, pre_recv, rs_send, rs_recv,
@@ -55,12 +55,6 @@
     def zb(by):
         return lax.rem(z + by + zs, zs)
 
-    barrier = pltpu.get_barrier_semaphore()
-    greeted = xdev[1:] + ydev[1:] + [sibling, zr, zl]
-    for dev in greeted:
-        pl.semaphore_signal(barrier, inc=1, device_id=dev, device_id_type=MESH)
-    pl.semaphore_wait(barrier, len(greeted))
-
     sent = []
 
     def send(src, dst, ssem, rsem, dev):
@@ -110,7 +104,7 @@
     def give(stage):
         for s in pair(stage):
             send(
-                source(s, 1 - k), w.at[s, y, x, half_rows(k)],
+                given_away.at[s], w.at[s, y, x, half_rows(k)],
                 give_send.at[s], give_recv.at[s], sibling,
             )
 
@@ -120,7 +114,7 @@
             for n, d in ((0, 1), (1, 3)):
                 at_n = 2 * n + k
                 send(
-                    source(s, k), part(s, i, j, k),
+                    part(s, i, j, k), part(s, i, j, k),
                     p1_send.at[s, at_n], p1_recv.at[s, at_n], first[d],
                 )
 
@@ -195,8 +189,7 @@
         for c in range(2):
             for n, to in ((0, zr), (1, zl)):
                 cc = c ^ n
-                src = tok_ref.at[:, pl.ds(256 * cc, 256)]
-                send(src, tok(0, cc), tok_send.at[n, 0, cc], tok_recv.at[n, 0, cc], to)
+                send(tok(0, cc), tok(0, cc), tok_send.at[n, 0, cc], tok_recv.at[n, 0, cc], to)
 
     def tok_forward(step):
         for c in range(2):
@@ -230,19 +223,11 @@
     def project_tokens(stage, places, first=False):
         add_chunks(stage, [2 * zb(by) + c for by in places for c in range(2)], first)
 
-    def project_rows(stage, yy, first=False):
-        add_chunks(stage, [4 * yy + i for i in range(4)], first)
-
-    def project_apart(stage, d, first=False):
-        for s in pair(stage):
-            j = turn(axes(s)[1], d)
-            cols = slice(HD * (s % 2), HD * (s % 2) + HD)
-            total = acc[stage, :, cols] if not first else None
-            for i in range(4):
-                at_f = (j, i) if s % 2 == 0 else (i, j)
-                value = mm(xs[4 * at_f[0] + at_f[1]], w[s, *at_f], 1, 0)
-                total = value if total is None else total + value
-            acc[stage, :, cols] = total
+    def project_places(stage, places, first=False):
+        add_chunks(stage, [4 * turn(y, dy) + turn(x, dx) for dy, dx in places], first)
+
+    near = [(dy, dx) for dy in (0, -1, 1) for dx in (0, -1, 1)]
+    far = [(2, dx) for dx in (0, -1, 1, 2)] + [(dy, 2) for dy in (0, -1, 1)]
 
     def piece(s):
         return acc[s // 2, :, (s % 2) * HD:(s % 2 + 1) * HD]
@@ -315,12 +300,26 @@
             for s in range(6)
         )
         yield from (
+            pltpu.make_async_copy(source(s, 1 - k), given_away.at[s], local_sem.at[8 + s])
+            for s in range(6)
+        )
+        yield from (
             pltpu.make_async_copy(
                 tok_ref.at[:, pl.ds(256 * c, 256)], tok(0, c), local_sem.at[6 + c]
             )
             for c in range(2)
         )
 
+    for copy in copies():
+        copy.start()
+    barrier = pltpu.get_barrier_semaphore()
+    greeted = xdev[1:] + ydev[1:] + [sibling, zr, zl]
+    for dev in greeted:
+        pl.semaphore_signal(barrier, inc=1, device_id=dev, device_id_type=MESH)
+    pl.semaphore_wait(barrier, len(greeted))
+
+    for copy in copies():
+        copy.wait()
     for stage in range(3):
         give(stage)
     p1_start(0)
@@ -330,10 +329,6 @@
     p1_given(1)
     p1_start(2)
     p1_given(2)
-    for copy in copies():
-        copy.start()
-    for copy in copies():
-        copy.wait()
     tok_share(0, 3)
     for stage in range(3):
         p1_forward(stage)
@@ -349,14 +344,14 @@
     tok_forward(2)
     p2_sides(0)
     p2_done(0)
-    tok_forward(3)
     tok_shared(0, 3)
     project_tokens(0, (0,), True)
+    tok_forward(3)
+    p2_forward(1)
+    p2_start(2, 0)
     tok_shared(-1, 5)
     tok_shared(1, 6)
     project_tokens(0, (-1,))
-    p2_forward(1)
-    p2_start(2, 0)
     project_tokens(0, (1,))
     tok_shared(-2, 7)
     tok_shared(2, 8)
@@ -371,24 +366,20 @@
     sum_one(0)
     p2_start(2, 1)
     p2_sides(1)
-    project_apart(1, 0, True)
-    project_apart(1, -1)
-    project_apart(1, 1)
+    project_places(1, near, True)
     p2_done(1)
-    project_apart(1, 2)
+    project_places(1, far)
     sums[1][0][...] = mm3(split(piece(KR)), split(piece(VR)), 0, 0)
     sum_one(1)
     p2_forward(2)
     share(KP, 0)
     share(VP, 1)
     sum_two(0, earlier)
-    project_apart(2, 0, True)
     p2_sides(2)
+    project_places(2, near, True)
     sum_two(1, earlier)
-    project_apart(2, -1)
-    project_apart(2, 1)
     p2_done(2)
-    project_apart(2, 2)
+    project_places(2, far)
     share(QP, 2)
 
     def causal(b):
@@ -396,15 +387,19 @@
         rows = lax.broadcasted_iota(jnp.int32, shape, 0) + 256 * b
         return rows >= lax.broadcasted_iota(jnp.int32, shape, 1)
 
-    for model, (qs, ks, vs) in enumerate(((QP, KP, VP), (QR, KR, VR))):
-        q, kk, v = (split(piece(s)) for s in (qs, ks, vs))
-        for b in range(2):
-            mine, upto = slice(256 * b, 256 * b + 256), slice(0, 256 * b + 256)
+    spans = [(slice(256 * b, 256 * b + 256), slice(0, 256 * b + 256)) for b in range(2)]
+    inner = {}
+    for model, (qs, ks) in enumerate(((QP, KP), (QR, KR))):
+        q, kk = split(piece(qs)), split(piece(ks))
+        for b, (mine, upto) in enumerate(spans):
             scores = mm3(cut(q, mine), cut(kk, upto), 1, 1)
-            scores = split(jnp.where(causal(b), scores, 0.0))
-            att[model, mine] = mm3(scores, cut(v, upto), 1, 0)
-            if model == 0:
-                sc[b, 0, :, upto], sc[b, 1, :, upto] = scores
+            inner[model, b] = split(jnp.where(causal(b), scores, 0.0))
+    for model, vs in enumerate((VP, VR)):
+        v = split(piece(vs))
+        for b, (mine, upto) in enumerate(spans):
+            att[model, mine] = mm3(inner[model, b], cut(v, upto), 1, 0)
+    for b, (_, upto) in enumerate(spans):
+        sc[b, 0, :, upto], sc[b, 1, :, upto] = inner[0, b]
     sum_three(0, earlier)
     att[0] += mm3(split(piece(QP)), result(0), 1, 0)
     sum_three(1, earlier)
@@ -417,8 +412,7 @@
     diff_ref[:, lanes(k)] = ed[core_rows(k)]
 
     q, kk, v, e = (split(a) for a in (piece(QP), piece(KP), piece(VP), ed[...]))
-    for b in range(2):
-        mine, upto = slice(256 * b, 256 * b + 256), slice(0, 256 * b + 256)
+    for b, (mine, upto) in enumerate(spans):
         weighted = mm3(cut(e, mine), cut(v, upto), 1, 1)
         weighted = split(jnp.where(causal(b), weighted, 0.0))
         scores = sc[b, 0, :, upto], sc[b, 1, :, upto]
@@ -438,32 +432,49 @@
         arrived(w2.at[at_n], sib_recv.at[at_n])
     sum_three(2, later)
     suffix = result(2)
-    g[1] = (scale * (att[0] + mm3(split(piece(VP)), suffix, 1, 1))).astype(BF16)
-    g[2] = (scale * (att[1] + mm3(split(piece(KP)), suffix, 1, 0))).astype(BF16)
+
+    def finish(kk):
+        rows = core_rows(kk)
+        keys, values = split(acc[0, rows, :HD]), split(acc[0, rows, HD:])
+        g[1, rows] = (scale * (att[0, rows] + mm3(values, suffix, 1, 1))).astype(BF16)
+        g[2, rows] = (scale * (att[1, rows] + mm3(keys, suffix, 1, 0))).astype(BF16)
+
+    finish(1 - k)
     theirs = g.at[pl.ds(1, 2), core_rows(1 - k)]
     send(theirs, gx.at[pl.ds(1, 2)], sib_send.at[13], sib_recv.at[13], sibling)
+    finish(k)
     arrived(gx.at[0], sib_recv.at[12])
+
+    def beside(left, right):
+        return jnp.concatenate([left, right], 1)
+
+    def rows_of(ref, at_s, h):
+        return ref[at_s, h // 2, pl.ds(2 * lax.rem(h, 2), 2)].reshape(512, HD)
+
+    def own_term(by, start, size):
+        h, few = zb(by), pl.ds(start, size)
+        own = pl.ds(pl.multiple_of(256 * k + start, 128), size)
+        return (
+            mm(beside(g[1, own], g[2, own]), beside(rows_of(w, KP, h), rows_of(w, VP, h)), 1, 1)
+            + mm(beside(g[0, own], gx[0, few]), beside(rows_of(w, QP, h), rows_of(w2, 2, h)), 1, 1)
+        )
+
+    def other_term(by, start, size):
+        h, few = zb(by), pl.ds(start, size)
+        return mm(beside(gx[1, few], gx[2, few]), beside(rows_of(w2, 0, h), rows_of(w2, 1, h)), 1, 1)
+
+    def term(by, half):
+        return own_term(by, 128 * half, 128) + other_term(by, 128 * half, 128)
+
+    opposite = own_term(4, 0, 256)
     arrived(gx.at[pl.ds(1, 2)], sib_recv.at[13])
-
-    def term(by, half):
-        h, few = zb(by), slice(128 * half, 128 * half + 128)
-        own = pl.ds(pl.multiple_of(256 * k + 128 * half, 128), 128)
-        at_h = (h // 2, pl.ds(2 * lax.rem(h, 2), 2))
-
-        def beside(left, right):
-            return jnp.concatenate([left, right], 1)
-
-        def rows_of(ref, at_s):
-            return ref[at_s, *at_h].reshape(512, HD)
-
-        return (
-            mm(beside(g[1, own], g[2, own]), beside(rows_of(w, KP), rows_of(w, VP)), 1, 1)
-            + mm(beside(gx[1, few], gx[2, few]), beside(rows_of(w2, 0), rows_of(w2, 1)), 1, 1)
-            + mm(beside(g[0, own], gx[0, few]), beside(rows_of(w, QP), rows_of(w2, 2)), 1, 1)
-        )
+    opposite = opposite + other_term(4, 0, 256)
 
     def hop(n, sign, out, inn, to, step, half):
-        value = term(sign * (5 - step), half)
+        if step == 1:
+            value = opposite[128 * half:128 * half + 128]
+        else:
+            value = term(sign * (5 - step), half)
         fresh = step == 1 or (step == 2 and half != n)
         if not fresh:
             arrived(inn.at[step - 2, half], rs_recv.at[n, step - 2, half])
@@ -482,9 +493,7 @@
                 if step == 1 and half != n:
                     continue
                 hop(n, sign, out, inn, to, step, half)
-    for half in range(2):
-        few = slice(128 * half, 128 * half + 128)
-        grad_ref[few] = term(0, half)
+    grad_ref[...] = own_term(0, 0, 256) + other_term(0, 0, 256)
     for turn_at in range(2):
         for n, _, _, inn, _ in ways:
             half = (1 - n) if turn_at == 0 else n
@@ -517,6 +526,7 @@
         scratch_shapes=[
             pltpu.VMEM((6, 4, 4, 256, HD), BF16),
             pltpu.VMEM((3, 4, 4, 256, HD), BF16),
+            pltpu.VMEM((6, 128, HD), BF16),
             pltpu.VMEM((16, 512, 256), BF16),
             pltpu.VMEM((3, 512, 2 * HD), F32),
             pltpu.VMEM((2, 512, HD), F32),
@@ -527,7 +537,7 @@
             pltpu.VMEM((3, 256, HD), BF16),
             (sums, sums, sums),
             half, half, half, half,
-            dma((8,)), dma((6,)), dma((6,)), dma((6, 6)), dma((6, 6)), dma((6, 6)), dma((6, 6)),
+            dma((14,)), dma((6,)), dma((6,)), dma((6, 6)), dma((6, 6)), dma((6, 6)), dma((6, 6)),
             dma((14,)), dma((14,)), dma((2, 4, 2)), dma((2, 4, 2)), dma((3, 12)), dma((3, 12)),
             dma((2, 4, 2)), dma((2, 4, 2)),
         ],

time: 92.2 us -> 91.7 us (level)
  no operation moved by 1% of the time
where the time goes in v4:
time: 91.7 us; the launch traced here: 91.6 us
  Pallas kernels  89.5 us (98%)
  local copies, waits for them, and re-layouts  1.5 us (2%)
    pallas_call x1, Pallas kernels, per_device(): pl.pallas_call(functools.partial(kernel, scale), out_shape=(pltpu.VMEM((2...  89.5 us

profile of v4, /device:TPU:1, one launch (start us, length us, event | category | flops | bytes accessed | tf_op | source)
XLA Modules:
  0.0 91.6 jit_solution(4105908406655532672)
XLA Ops:
  0.6 89.5 %shard_map.50 = (f32[256,256]{1,0:T(8,128)S(1)}, f32[256,512]{1,0:T(8,128)S(1)}) custom-call(bf16[256,512]{1,0:T(8,128)(2,1)} %tok_ref.1, bf16[3,128,256]{2,1,0:T(8,128)(2,1)} %pol_ref.1, bf16[3,128,256]{2,1,0:T(8,128)(2,1)} %ref_ref.1), custom_call_target="tpu_custom_call" | custom-call | tf_op jit(solution)/shard_map/pallas_call | solution.py:518
  90.1 0.7 copy.7
  90.8 0.8 copy.8

commit v5 on v4

--- a/solution.py
+++ b/solution.py
@@ -250,21 +250,24 @@
         partial = jnp.zeros_like(total)
         ahead = jnp.zeros_like(total)
         for d in (1, 3, 2):
-            at_x, at_y = turn(x, -d), turn(y, -d)
+            at_x = turn(x, -d)
             arrived(got1.at[0, at_x], pre_recv.at[t, d - 1])
             value = got1[0, at_x]
             total += value
             partial += jnp.where(before(at_x, x), value, 0.0)
-            arrived(got1.at[1, at_y], pre_recv.at[t, 2 + d])
-            ahead += jnp.where(before(at_y, y), got1[1, at_y], 0.0)
         msg[0] = total
-        msg[1] = ahead
-        msg[2] = ahead + chip[64:]
         for d in (2, 1, 3):
             send(
                 msg.at[0], got2.at[0, y],
                 pre_send.at[t, 5 + d], pre_recv.at[t, 5 + d], ydev[d],
             )
+        for d in (1, 3, 2):
+            at_y = turn(y, -d)
+            arrived(got1.at[1, at_y], pre_recv.at[t, 2 + d])
+            ahead += jnp.where(before(at_y, y), got1[1, at_y], 0.0)
+        msg[1] = ahead
+        msg[2] = ahead + chip[64:]
+        for d in (2, 1, 3):
             which = jnp.where(before(x, turn(x, d)), 2, 1)
             send(
                 msg.at[which], got2.at[1, x],
@@ -433,16 +436,16 @@
     sum_three(2, later)
     suffix = result(2)
 
-    def finish(kk):
+    def finish(kk, give_away):
         rows = core_rows(kk)
-        keys, values = split(acc[0, rows, :HD]), split(acc[0, rows, HD:])
-        g[1, rows] = (scale * (att[0, rows] + mm3(values, suffix, 1, 1))).astype(BF16)
-        g[2, rows] = (scale * (att[1, rows] + mm3(keys, suffix, 1, 0))).astype(BF16)
-
-    finish(1 - k)
-    theirs = g.at[pl.ds(1, 2), core_rows(1 - k)]
-    send(theirs, gx.at[pl.ds(1, 2)], sib_send.at[13], sib_recv.at[13], sibling)
-    finish(k)
+        for c, cols, turned in ((1, slice(HD, None), 1), (2, slice(HD), 0)):
+            value = mm3(split(acc[0, rows, cols]), suffix, 1, turned)
+            g[c, rows] = (scale * (att[c - 1, rows] + value)).astype(BF16)
+            if give_away:
+                send(g.at[c, rows], gx.at[c], sib_send.at[12 + c], sib_recv.at[12 + c], sibling)
+
+    finish(1 - k, True)
+    finish(k, False)
     arrived(gx.at[0], sib_recv.at[12])
 
     def beside(left, right):
@@ -467,7 +470,8 @@
         return own_term(by, 128 * half, 128) + other_term(by, 128 * half, 128)
 
     opposite = own_term(4, 0, 256)
-    arrived(gx.at[pl.ds(1, 2)], sib_recv.at[13])
+    arrived(gx.at[1], sib_recv.at[13])
+    arrived(gx.at[2], sib_recv.at[14])
     opposite = opposite + other_term(4, 0, 256)
 
     def hop(n, sign, out, inn, to, step, half):
@@ -538,7 +542,7 @@
             (sums, sums, sums),
             half, half, half, half,
             dma((14,)), dma((6,)), dma((6,)), dma((6, 6)), dma((6, 6)), dma((6, 6)), dma((6, 6)),
-            dma((14,)), dma((14,)), dma((2, 4, 2)), dma((2, 4, 2)), dma((3, 12)), dma((3, 12)),
+            dma((15,)), dma((15,)), dma((2, 4, 2)), dma((2, 4, 2)), dma((3, 12)), dma((3, 12)),
             dma((2, 4, 2)), dma((2, 4, 2)),
         ],
         compiler_params=pltpu.CompilerParams(

time: 91.7 us -> 91.9 us (level)
  no operation moved by 1% of the time
where the time goes in v5:
time: 91.9 us; the launch traced here: 91.8 us
  Pallas kernels  89.7 us (98%)
  local copies, waits for them, and re-layouts  1.5 us (2%)
    pallas_call x1, Pallas kernels, per_device(): pl.pallas_call(functools.partial(kernel, scale), out_shape=(pltpu.VMEM((2...  89.7 us

profile of v5, /device:TPU:1, one launch (start us, length us, event | category | flops | bytes accessed | tf_op | source)
XLA Modules:
  0.0 91.8 jit_solution(5005615554053402859)
XLA Ops:
  0.6 89.7 %shard_map.50 = (f32[256,256]{1,0:T(8,128)S(1)}, f32[256,512]{1,0:T(8,128)S(1)}) custom-call(bf16[256,512]{1,0:T(8,128)(2,1)} %tok_ref.1, bf16[3,128,256]{2,1,0:T(8,128)(2,1)} %pol_ref.1, bf16[3,128,256]{2,1,0:T(8,128)(2,1)} %ref_ref.1), custom_call_target="tpu_custom_call" | custom-call | tf_op jit(solution)/shard_map/pallas_call | solution.py:522
  90.3 0.7 copy.7
  91.0 0.8 copy.8
